TPU v7x, 32 devices: a whole 2x2x4 slice. The times are simulated.
32 devices in a mesh: dp: 4 (over z), ctx: 2 (over x), head: 4 (over y, core).
Axes of the slice: x: 2, y: 2, z: 4, core: 2. Of those that a mesh axis runs over, the one named last changes fastest.
Arguments:
- queries: bfloat16 [4, 256, 64, 288], P('dp', 'ctx', 'head'), may hold values from -100 to 100
- latents: bfloat16 [4, 256, 288], P('dp', 'ctx'), may hold values from -16 to 16
- positions: int32 [4, 256], P('dp', 'ctx'), may hold values from 0 to 255, as said below
- lse: float32 [4, 256, 64], P('dp', 'ctx', 'head'), as said below
- saved_out: bfloat16 [4, 256, 64, 256], P('dp', 'ctx', 'head'), may hold values from -6 to 6
- out_grad: bfloat16 [4, 256, 64, 128], P('dp', 'ctx', 'head'), may hold values from -6 to 6
- value_up: bfloat16 [64, 256, 128], P('head'), may hold values from -0.375 to 0.375
Outputs:
- query_grad: bfloat16 [4, 256, 64, 288], P('dp', 'ctx', 'head')
- latent_grad: float32 [4, 256, 288], P('dp', 'ctx')
- value_up_grad: float32 [256, 64, 128], P(('dp', 'ctx'), 'head')
Inputs may be any that keep to these rules, and one draw needn't show every extreme that they name: For each sequence the 256 positions are a permutation of 0 to 255; the 128 slots of each aligned block of 128 slots hold 128 consecutive positions, beginning at a multiple of 128, in some order. lse[b, i, h] is the logarithm of the sum over the slots j visible to i of exp(logits[i, j]).
All inputs are finite; a program needn't handle non-finite values.
Results may differ from a plain program's by a relative error of at most 0.014.
Values may be sent and summed in bfloat16 or wider, within the bound.
A program may use at most 64 MiB of HBM per device.

v0:
```python
import jax
import jax.numpy as jnp
from jax import lax
from jax.sharding import PartitionSpec as P

ROPE = 32
VHEAD = 128


def spans(length):
    return [(lower, min(length, lower + 512)) for lower in range(0, length, 512)]


def body(queries, latents, positions, lse, saved_out, out_grad, value_up):
    query_rows = queries[0]
    slot_count = query_rows.shape[0]
    head_count = query_rows.shape[1]
    full_width = query_rows.shape[2]
    latent_width = saved_out.shape[3]
    query_pos = positions[0]
    row_lse = lse[0]
    latest = jnp.max(query_pos)
    scaling = (VHEAD + ROPE) ** (-0.5)
    lat_grad = jnp.einsum(
        "thv,hlv->thl", out_grad[0], value_up, preferred_element_type=jnp.float32
    ).astype(jnp.bfloat16)
    row_delta = jnp.sum(lat_grad.astype(jnp.float32) * saved_out[0].astype(jnp.float32), axis=-1)
    slab_rows = slot_count * lax.axis_size("ctx")
    grad_init = (
        jnp.zeros((slot_count, head_count, full_width), jnp.float32),
        jnp.zeros((slab_rows, full_width), jnp.float32),
    )
    carry = grad_init
    keys_in = lax.all_gather(latents[0], "ctx", axis=0, tiled=True)
    pos_in = lax.all_gather(positions[0], "ctx", axis=0, tiled=True)
    for lower, upper in spans(keys_in.shape[0]):
        key_rows = keys_in[lower:upper]
        key_pos = pos_in[lower:upper]

        def update(state):
            query_acc, key_acc = state
            logits = (
                jnp.einsum("thd,kd->thk", query_rows, key_rows, preferred_element_type=jnp.float32)
                * scaling
            )
            visible = key_pos[None, None, :] <= query_pos[:, None, None]
            weights = jnp.where(visible, jnp.exp(logits - row_lse[:, :, None]), 0.0)
            dot_value = jnp.einsum(
                "thl,kl->thk",
                lat_grad,
                key_rows[:, :latent_width],
                preferred_element_type=jnp.float32,
            )
            dlogits = (weights * (dot_value - row_delta[:, :, None]) * scaling).astype(jnp.bfloat16)
            query_acc = query_acc + jnp.einsum(
                "thk,kd->thd", dlogits, key_rows, preferred_element_type=jnp.float32
            )
            key_term = jnp.einsum(
                "thk,thd->kd", dlogits, query_rows, preferred_element_type=jnp.float32
            )
            value_term = jnp.einsum(
                "thk,thl->kl",
                weights.astype(jnp.bfloat16),
                lat_grad,
                preferred_element_type=jnp.float32,
            )
            key_term = key_term + jnp.pad(value_term, ((0, 0), (0, full_width - latent_width)))
            previous = lax.dynamic_slice_in_dim(key_acc, 0 + lower, upper - lower, 0)
            key_acc = lax.dynamic_update_slice_in_dim(key_acc, previous + key_term, 0 + lower, 0)
            return (query_acc, key_acc)

        carry = lax.cond(jnp.min(key_pos) > latest, lambda state: state, update, carry)
    query_acc, key_acc = carry
    summed = lax.psum(key_acc, "head")
    own_rows = lax.psum_scatter(summed, "ctx", scatter_dimension=0, tiled=True)
    saved_part = saved_out[0]
    weight_share = lax.psum_scatter(
        jnp.einsum("thl,thv->lhv", saved_part, out_grad[0], preferred_element_type=jnp.float32),
        ("dp", "ctx"),
        scatter_dimension=0,
        tiled=True,
    )
    return (query_acc.astype(jnp.bfloat16)[None], own_rows[None], weight_share)


def solution(mesh):
    return jax.shard_map(
        body,
        mesh=mesh,
        in_specs=(
            P("dp", "ctx", "head", None),
            P("dp", "ctx", None),
            P("dp", "ctx"),
            P("dp", "ctx", "head"),
            P("dp", "ctx", "head", None),
            P("dp", "ctx", "head", None),
            P("head", None, None),
        ),
        out_specs=(
            P("dp", "ctx", "head", None),
            P("dp", "ctx", None),
            P(("dp", "ctx"), "head", None),
        ),
        check_vma=False,
    )
```

profile of v0, /device:TPU:0, one launch (start us, length us, event | category | flops | bytes accessed | tf_op | source)
XLA Modules:
  0.0 133.3 jit_solution(2473021390927511355)
XLA Ops:
  8.0 0.0 copy-start
  8.0 0.0 reduce-scatter.5.cloned.1.call-start
  8.1 5.4 %all-gather = s32[1,256]{1,0:T(1,128)S(1)} all-gather(s32[1,128]{1,0:T(1,128)} %param.11), channel_id=2, replica_groups=mesh['dp'=4,'ctx'=2,'head'=4] {'ctx'}, dimensions={1}, use_global_device_ids=true | all-gather | bytes 1536 | tf_op jit(solution)/shard_map/all_gather | solution.py:35
  13.5 1.3 reduce_max.9
  14.8 0.6 reduce_min.9
  16.7 1.0 copy.25
  17.7 5.3 %all-gather.1 = bf16[1,256,288]{2,1,0:T(8,128)(2,1)S(1)} all-gather(bf16[1,128,288]{2,1,0:T(8,128)(2,1)S(1)} %copy.25), channel_id=3, replica_groups=mesh['dp'=4,'ctx'=2,'head'=4] {'ctx'}, dimensions={1}, use_global_device_ids=true | all-gather | bytes 221184 | tf_op jit(solution)/shard_map/all_gather | solution.py:34
  23.0 1.5 %copy.28 = bf16[128,16,128]{0,2,1:T(8,128)(2,1)S(1)} copy(bf16[128,16,128]{2,1,0:T(8,128)(2,1)} %bitcast.49) | data formatting | bytes 1048576 | tf_op jit(solution)/shard_map/squeeze | solution.py:25
  24.5 0.0 copy-done
  24.5 0.0 copy-start.1
  24.5 0.0 copy-start.4
  24.5 0.0 copy-start.6
  24.5 1.8 %fusion.17 = (f32[128,16,256]{0,2,1:T(8,128)}, bf16[128,16,256]{0,2,1:T(8,128)(2,1)S(1)}) fusion(bf16[16,256,128]{2,1,0:T(8,128)(2,1)S(1)} %copy-done, bf16[128,16,128]{0,2,1:T(8,128)(2,1)S(1)} %copy.28), kind=kOutput, calls=%fused_computation.21 | convolution fusion | flops 135266304 | bytes 4718592 | tf_op jit(solution)/shard_map/thv,hlv->thl/dot_general | solution.py:24
  26.3 0.0 copy-done.4
  26.3 0.0 copy-done.6
  26.3 0.0 copy-done.1
  26.3 10.5 %conditional.1 = (bf16[128,16,288]{0,2,1:T(8,128)(2,1)S(1)}, f32[256,288]{0,1:T(8,128)S(1)}) conditional(s32[]{:T(128)} %convert_element_type.30, (s32[256]{0:T(256)S(1)}, s32[1,128]{1,0:T(1,128)S(1)}, bf16[1,128,16,288]{1,3,2,0:T(8,128)(2,1)}, bf16[256,288]{1,0:T(8,128)(2,1)S(1)}, f32[1,128,16]{1,2,0:T(8,128)S(1)}, ...), branch_computations={%region_2.4_spmd, %region_4.5_spmd} | conditional | flops 1448712192 | bytes 28485164 | solution.py:72
  26.3 3.1 %copy.27 = f32[128,16,256]{2,1,0:T(8,128)} copy(f32[128,16,256]{0,2,1:T(8,128)} %get-tuple-element.74) | data formatting | bytes 4194304 | tf_op jit(solution)/shard_map
  29.4 2.2 %multiply_reduce_fusion = f32[128,16]{1,0:T(8,128)S(1)} fusion(f32[128,16,256]{2,1,0:T(8,128)} %copy.27, bf16[128,16,256]{2,1,0:T(8,128)(2,1)} %get-tuple-element.44), kind=kLoop, calls=%fused_computation.1 | loop fusion | flops 1570816 | bytes 3153920 | tf_op jit(solution)/shard_map/reduce_sum | solution.py:27
  31.6 0.1 copy.23
  31.7 0.1 broadcast_compare_fusion
  31.8 2.3 %exponential_select_fusion = f32[128,16,256]{2,0,1:T(8,128)S(1)} fusion(bf16[1,128,16,288]{1,3,2,0:T(8,128)(2,1)} %get-tuple-element.54, f32[128,16]{0,1:T(8,128)S(1)} %bitcast.53, pred[128,256]{1,0:T(8,128)(4,1)S(1)} %broadcast_compare_fusion, bf16[256,288]{1,0:T(8,128)(2,1)S(1)} %get-tuple-element.40), kind=kOutput, calls=%fused_computation.2 | convolution fusion | flops 303562752 | bytes 3465216 | tf_op jit(solution)/shard_map/cond/branch_0_fun/thd,kd->thk/dot_general | solution.py:43
  34.1 0.5 convolution_bitcast_fusion
  34.6 0.0 copy-start.5
  34.6 0.7 multiply_convert_fusion
  35.3 0.5 copy-done.5
  35.9 0.5 fusion.6
  36.3 0.5 fusion.10
  36.9 0.0 copy-start.3
  36.9 0.0 copy-start.2
  36.9 0.7 copy-done.3
  37.6 0.0 reduce-scatter.5.cloned.1.call-update
  37.6 0.0 all-reduce.3.cloned.1.call-start
  37.6 13.9 %reduce-scatter.5.cloned.1.call-done = f32[128,288]{0,1:T(8,128)} async-done(((f32[256,288]{0,1:T(8,128)}), f32[128,288]{0,1:T(8,128)}) %reduce-scatter.5.cloned.1.call-update) | async-done | bytes 147472 | tf_op jit(solution)/shard_map/reduce_scatter | solution.py:75
  51.5 0.0 all-reduce.3.cloned.1.call-update
  51.5 0.0 copy-done.2
  51.6 0.0 reduce-scatter.3.cloned.1.call-start
  51.6 1.9 %convolution_bitcast_fusion.1 = f32[256,16,128]{0,2,1:T(8,128)S(1)} fusion(bf16[128,16,128]{0,2,1:T(8,128)(2,1)} %copy-done.1, bf16[128,16,256]{2,1,0:T(8,128)(2,1)} %bitcast.46), kind=kOutput, calls=%fused_computation.16 | convolution fusion | flops 134217728 | bytes 3670016 | tf_op jit(solution)/shard_map/thl,thv->lhv/dot_general | solution.py:78
  53.5 2.0 %copy.30 = f32[256,16,128]{2,1,0:T(8,128)} copy(f32[256,16,128]{0,2,1:T(8,128)S(1)} %convolution_bitcast_fusion.1) | data formatting | bytes 4194304 | tf_op jit(solution)/shard_map/thl,thv->lhv/transpose | solution.py:78
  55.5 0.0 reduce-scatter.3.cloned.1.call-update
  55.6 29.2 %all-reduce.3.cloned.1.call-done = f32[128,288]{0,1:T(8,128)} async-done(((f32[128,288]{0,1:T(8,128)}), f32[128,288]{0,1:T(8,128)}) %all-reduce.3.cloned.1.call-update) | async-done | bytes 147472 | tf_op jit(solution)/shard_map/psum | solution.py:74
  84.7 39.5 %reduce-scatter.3.cloned.1.call-done = f32[32,16,128]{2,1,0:T(8,128)} async-done(((f32[256,16,128]{2,1,0:T(8,128)}), f32[32,16,128]{2,1,0:T(8,128)}) %reduce-scatter.3.cloned.1.call-update) | async-done | bytes 262160 | tf_op jit(solution)/shard_map/reduce_scatter | solution.py:77
  124.2 1.6 %copy.43 = f32[1,128,288]{1,2,0:T(8,128)} copy(f32[1,128,288]{1,2,0:T(8,128)} %bitcast.50) | data formatting | bytes 294912
Async XLA Ops:
  8.0 16.5 %copy-start = (bf16[16,256,128]{2,1,0:T(8,128)(2,1)S(1)}, bf16[16,256,128]{2,1,0:T(8,128)(2,1)}, u32[]{:S(2)}) copy-start(bf16[16,256,128]{2,1,0:T(8,128)(2,1)} %param.15) | copy-start | bytes 3145732
  8.0 43.5 %reduce-scatter.5.cloned.1.call-start = ((), (), s32[]{:S(2)}) async-start(), calls=%async_computation.3 | async-start | bytes 442368 | tf_op jit(solution)/shard_map/reduce_scatter | solution.py:75
  24.5 1.8 %copy-start.1 = (bf16[128,16,128]{0,2,1:T(8,128)(2,1)}, bf16[128,16,128]{0,2,1:T(8,128)(2,1)S(1)}, u32[]{:S(2)}) copy-start(bf16[128,16,128]{0,2,1:T(8,128)(2,1)S(1)} %copy.28) | copy-start | bytes 1572868
  24.5 1.8 %copy-start.4 = (s32[1,128]{1,0:T(1,128)S(1)}, s32[1,128]{1,0:T(1,128)}, u32[]{:S(2)}) copy-start(s32[1,128]{1,0:T(1,128)} %param.11) | copy-start | bytes 1540
  24.5 1.8 %copy-start.6 = (f32[1,128,16]{1,2,0:T(8,128)S(1)}, f32[1,128,16]{1,2,0:T(8,128)}, u32[]{:S(2)}) copy-start(f32[1,128,16]{1,2,0:T(8,128)} %param.12) | copy-start | bytes 24580
  34.6 1.3 copy-start.5
  36.9 0.7 copy-start.3
  36.9 14.7 %copy-start.2 = (bf16[128,16,288]{0,2,1:T(8,128)(2,1)}, bf16[128,16,288]{0,2,1:T(8,128)(2,1)S(1)}, u32[]{:S(2)}) copy-start(bf16[128,16,288]{0,2,1:T(8,128)(2,1)S(1)} %get-tuple-element.50) | copy-start | bytes 3538948
  37.6 47.1 %all-reduce.3.cloned.1.call-start = ((), (), s32[]{:S(2)}) async-start(), calls=%async_computation.4 | async-start | bytes 294912 | tf_op jit(solution)/shard_map/psum | solution.py:74
  51.6 72.7 %reduce-scatter.3.cloned.1.call-start = ((), (), s32[]{:S(2)}) async-start(), calls=%async_computation.2 | async-start | bytes 2359296 | tf_op jit(solution)/shard_map/reduce_scatter | solution.py:77
Sparse Core Ops, SparseCore 0:
  37.7 13.7 reduce-scatter.4
  53.9 30.8 all-reduce.2
Sparse Core Ops, SparseCore 1:
  56.5 67.6 reduce-scatter.2
where the time goes:
time: 134 us; the launch traced here: 133 us
  waiting for transfers between devices  82.6 us (62%)
  between operations  16.9 us (13%)
  blocking collectives  10.7 us (8%)
  local copies, waits for them, and re-layouts  10.4 us (8%)
  matrix products  8.16 us (6%)
  other arithmetic  4.24 us (3%)
    reduce_scatter x1, waiting for transfers between devices, body(): lax.psum_scatter(jnp.einsum('thl,thv->lhv', saved_part, out_grad[0], pref...  39.5 us
    psum x1, waiting for transfers between devices, body(): summed = lax.psum(key_acc, 'head')  29.2 us
    reduce_scatter x1, waiting for transfers between devices, body(): own_rows = lax.psum_scatter(summed, 'ctx', scatter_dimension=0, tiled=True)  13.9 us
    all_gather x1, blocking collectives, body(): pos_in = lax.all_gather(positions[0], 'ctx', axis=0, tiled=True)  5.44 us
    all_gather x1, blocking collectives, body(): keys_in = lax.all_gather(latents[0], 'ctx', axis=0, tiled=True)  5.29 us
    unnamed x14, local copies, waits for them, and re-layouts  3.29 us
    another operation x1, local copies, waits for them, and re-layouts  3.1 us
  transfers between devices with their start and end apart: 3, of which 3 were waited for; matrix products, arithmetic and copies ran while one was open for 3% of the time, Pallas kernels for 0%

commit v1 on v0

--- a/solution.py
+++ b/solution.py
@@ -1,17 +1,330 @@
+import functools
+
 import jax
 import jax.numpy as jnp
 from jax import lax
+from jax.experimental import pallas as pl
+from jax.experimental.pallas import tpu as pltpu
 from jax.sharding import PartitionSpec as P
 
 ROPE = 32
 VHEAD = 128
+MESH = pl.DeviceIdType.MESH
+BF16 = jnp.bfloat16
+F32 = jnp.float32
+CHUNKS = 4
+
+
+def dot(lhs, rhs, over):
+    return lax.dot_general(lhs, rhs, (((over[0],), (over[1],)), ((), ())), preferred_element_type=F32)
+
+
+def kernel(
+    dims,
+    q_hbm, lat_hbm, pos_hbm, lse_hbm, saved_hbm, grad_hbm, up_hbm,
+    qg_hbm, lg_out, vg_out,
+    q_ref, kt_in, pos_in, lse_ref, saved_b, grad_b, up_ref,
+    saved_lo, saved_hi, grad_f, saved_h, grad_h,
+    keys, keys_t, bias,
+    vx, vr, zs, zr,
+    key_acc, ka_send, ka_recv, kb_send, kb_recv, kc,
+    qg_ref,
+    in_sem, lat_send, lat_recv, x_send, x_recv, z_send, z_recv,
+    ka_ssem, ka_rsem, kb_sem, kc_ssem, kc_rsem, out_sem,
+):
+    n_dp, n_head, heads, slots, width, latent, share = dims
+    scaling = (VHEAD + ROPE) ** -0.5
+    my_dp, my_ctx, my_head = lax.axis_index("dp"), lax.axis_index("ctx"), lax.axis_index("head")
+    other = 1 - my_ctx
+    per_chunk = heads // CHUNKS
+    piece = key_acc.shape[0] // n_head
+
+    def load(index, source, target):
+        copy = pltpu.make_async_copy(source, target, in_sem.at[index])
+        copy.start()
+        return copy
+
+    lat_in = load(0, lat_hbm, kt_in.at[my_ctx])
+    pos_load = load(1, pos_hbm, pos_in.at[my_ctx])
+    saved_in = load(2, saved_hbm, saved_b)
+    grad_in = load(3, grad_hbm, grad_b)
+    up_in = load(4, up_hbm, up_ref)
+    q_in = load(5, q_hbm, q_ref)
+    lse_in = load(6, lse_hbm, lse_ref)
+
+    barrier = pltpu.get_barrier_semaphore()
+    pl.semaphore_signal(barrier, inc=1, device_id={"ctx": other}, device_id_type=MESH)
+    for step in range(1, n_dp):
+        pl.semaphore_signal(barrier, inc=1, device_id={"dp": lax.rem(my_dp + step, n_dp)}, device_id_type=MESH)
+    for step in range(1, n_head):
+        pl.semaphore_signal(barrier, inc=1, device_id={"head": lax.rem(my_head + step, n_head)}, device_id_type=MESH)
+    lat_in.wait()
+    pos_load.wait()
+    pl.semaphore_wait(barrier, 1 + (n_dp - 1) + (n_head - 1))
+
+    def send(source, target, send_sem, recv_sem, where):
+        return pltpu.make_async_remote_copy(
+            src_ref=source, dst_ref=target, send_sem=send_sem, recv_sem=recv_sem,
+            device_id=where, device_id_type=MESH)
+
+    lat_copy = send(kt_in.at[my_ctx], kt_in.at[my_ctx], lat_send.at[0], lat_recv.at[0], {"ctx": other})
+    pos_copy = send(pos_in.at[my_ctx], pos_in.at[my_ctx], lat_send.at[1], lat_recv.at[1], {"ctx": other})
+    lat_copy.start()
+    pos_copy.start()
+
+    saved_in.wait()
+    grad_in.wait()
+    rows_step = (slots * heads) // 8
+
+    def widen(step, carry):
+        rows = pl.ds(pl.multiple_of(step * rows_step, rows_step), rows_step)
+        saved_lo[rows, :] = saved_b[rows, :128].astype(F32)
+        saved_hi[rows, :] = saved_b[rows, 128:].astype(F32)
+        grad_f[rows, :] = grad_b[rows, :].astype(F32)
+        return carry
+
+    lax.fori_loop(0, 8, widen, 0)
+
+    def up_partial(head, carry):
+        rows = pl.ds(head, slots, heads)
+        low = saved_lo[rows, :].astype(BF16)
+        high = saved_hi[rows, :].astype(BF16)
+        grad = grad_f[rows, :].astype(BF16)
+        saved_h[head, :, :128] = low
+        saved_h[head, :, 128:] = high
+        grad_h[head] = grad
+        product = jnp.concatenate([dot(low, grad, (0, 0)), dot(high, grad, (0, 0))], axis=0).astype(BF16)
+        for dp in range(n_dp):
+            for ctx in range(2):
+                first = (dp * 2 + ctx) * share
+                vx[ctx, head, dp] = product[first:first + share]
+        return carry
+
+    x_copies = []
+    for chunk in range(CHUNKS):
+        lax.fori_loop(chunk * per_chunk, (chunk + 1) * per_chunk, up_partial, 0)
+        part = pl.ds(chunk * per_chunk, per_chunk)
+        copy = send(vx.at[other, part], vr.at[part], x_send.at[chunk], x_recv.at[chunk], {"ctx": other})
+        copy.start()
+        x_copies.append(copy)
+
+    lat_copy.wait_recv()
+    pos_copy.wait_recv()
+    query_pos = pos_in[my_ctx]
+    for half in range(2):
+        cols = slice(half * slots, (half + 1) * slots)
+        block = kt_in[half]
+        keys_t[:, cols] = block
+        keys[cols, :] = block.astype(F32).T.astype(BF16)
+        key_pos = jnp.broadcast_to(pos_in[half], (slots, slots)).T
+        bias[cols, :] = jnp.where(key_pos <= query_pos, 0.0, -1e30)
+    key_acc[...] = jnp.zeros_like(key_acc)
+    up_in.wait()
+    q_in.wait()
+    lse_in.wait()
+    diagonal = lax.broadcasted_iota(jnp.int32, (slots, slots), 0) == lax.broadcasted_iota(
+        jnp.int32, (slots, slots), 1)
+
+    def attend(pair, carry):
+        one, two = 2 * pair, 2 * pair + 1
+        lat_grads, deltas = [], []
+        for head in (one, two):
+            lat_grad = dot(up_ref[head], grad_h[head], (1, 1)).astype(BF16)
+            lat_grads.append(lat_grad)
+            full = dot(saved_h[head], lat_grad, (1, 0))
+            deltas.append(jnp.sum(jnp.where(diagonal, full, 0.0), axis=0, keepdims=True))
+        lat_grad = jnp.concatenate(lat_grads, axis=1)
+        delta = jnp.concatenate(deltas, axis=1)
+        query = jnp.concatenate([q_ref[one], q_ref[two]], axis=1)
+        lse = jnp.concatenate([lse_ref[pl.ds(one, 1), :], lse_ref[pl.ds(two, 1), :]], axis=1)
+        mask = jnp.concatenate([bias[...], bias[...]], axis=1)
+        logits = dot(keys[...], query, (1, 0)) * scaling
+        weights = jnp.exp(logits - lse + mask)
+        dot_value = dot(keys[:, :latent], lat_grad, (1, 0))
+        dlogits = (weights * (dot_value - delta) * scaling).astype(BF16)
+        weights_b = weights.astype(BF16)
+        query_grad = dot(keys_t[...], dlogits, (1, 0)).astype(BF16)
+        qg_ref[one] = query_grad[:, :slots]
+        qg_ref[two] = query_grad[:, slots:]
+        key_term = dot(query, dlogits, (1, 1))
+        value_term = dot(lat_grad, weights_b, (1, 1))
+        key_acc[:latent, :] += key_term[:latent] + value_term
+        key_acc[latent:width, :] += key_term[latent:]
+        return carry
+
+    z_copies = []
+
+    def forward(chunk):
+        x_copies[chunk].wait_recv()
+
+        def add(head, carry):
+            for dp in range(n_dp):
+                zs[dp, head] = (vx[my_ctx, head, dp].astype(F32) + vr[head, dp].astype(F32)).astype(BF16)
+            return carry
+
+        lax.fori_loop(chunk * per_chunk, (chunk + 1) * per_chunk, add, 0)
+        part = pl.ds(chunk * per_chunk, per_chunk)
+        for step in range(1, n_dp):
+            to = lax.rem(my_dp + step, n_dp)
+            copy = send(zs.at[to, part], zr.at[my_dp, part], z_send.at[to, chunk], z_recv.at[my_dp, chunk], {"dp": to})
+            copy.start()
+            z_copies.append(copy)
+
+    def attend_chunk(chunk):
+        lax.fori_loop(chunk * per_chunk // 2, (chunk + 1) * per_chunk // 2, attend, 0)
+
+    attend_chunk(0)
+    attend_chunk(1)
+    forward(0)
+    attend_chunk(2)
+    attend_chunk(3)
+    qg_copy = pltpu.make_async_copy(qg_ref, qg_hbm, out_sem)
+    qg_copy.start()
+
+    for part in range(n_head):
+        for ctx in range(2):
+            ka_send[part, ctx] = key_acc[
+                part * piece:(part + 1) * piece, ctx * slots:(ctx + 1) * slots].astype(BF16)
+    ka_copies = []
+    for step in range(1, n_head):
+        to = lax.rem(my_head + step, n_head)
+        copy = send(ka_send.at[to], ka_recv.at[my_head], ka_ssem.at[to], ka_rsem.at[my_head], {"head": to})
+        copy.start()
+        ka_copies.append(copy)
+
+    forward(1)
+
+    sums = ka_send[my_head].astype(F32)
+    for step in range(1, n_head):
+        src = lax.rem(my_head + step, n_head)
+        send(ka_send.at[src], ka_recv.at[src], ka_ssem.at[src], ka_rsem.at[src], {"head": src}).wait_recv()
+        sums = sums + ka_recv[src].astype(F32)
+    kb_send[...] = sums.astype(BF16)
+    kb_copy = send(kb_send.at[other], kb_recv, kb_sem.at[0], kb_sem.at[1], {"ctx": other})
+    kb_copy.start()
+
+    forward(2)
+
+    kb_copy.wait_recv()
+    kc[my_head] = (kb_send[my_ctx].astype(F32) + kb_recv[...].astype(F32)).astype(BF16)
+    kc_copies = []
+    for step in range(1, n_head):
+        to = lax.rem(my_head + step, n_head)
+        copy = send(kc.at[my_head], kc.at[my_head], kc_ssem.at[to], kc_rsem.at[my_head], {"head": to})
+        copy.start()
+        kc_copies.append(copy)
+
+    forward(3)
+
+    for step in range(1, n_head):
+        src = lax.rem(my_head + step, n_head)
+        send(kc.at[src], kc.at[src], kc_ssem.at[src], kc_rsem.at[src], {"head": src}).wait_recv()
+    for part in range(n_head):
+        first, last = part * piece, min((part + 1) * piece, width)
+        lg_out[first:last, :] = kc[part, :last - first, :].astype(F32)
+
+    def finish(head, carry):
+        total = zs[my_dp, head].astype(F32)
+        for step in range(1, n_dp):
+            total = total + zr[lax.rem(my_dp + step, n_dp), head].astype(F32)
+        vg_out[pl.ds(head, share, heads), :] = total
+        return carry
+
+    for chunk in range(CHUNKS):
+        part = pl.ds(chunk * per_chunk, per_chunk)
+        for step in range(1, n_dp):
+            src = lax.rem(my_dp + step, n_dp)
+            send(zs.at[src, part], zr.at[src, part], z_send.at[src, chunk], z_recv.at[src, chunk],
+                 {"dp": src}).wait_recv()
+        lax.fori_loop(chunk * per_chunk, (chunk + 1) * per_chunk, finish, 0)
+
+    for copy in [lat_copy, pos_copy, kb_copy] + x_copies + z_copies + ka_copies + kc_copies:
+        copy.wait_send()
+    qg_copy.wait()
+
+
+def fused(mesh, queries, latents, positions, lse, saved_out, out_grad, value_up):
+    n_dp, n_head = mesh.shape["dp"], mesh.shape["head"]
+    _, slots, heads, width = queries.shape
+    latent = saved_out.shape[3]
+    vhead = out_grad.shape[3]
+    share = latent // (n_dp * 2)
+    unit = 16 * n_head
+    piece = -(-width // unit) * 16
+    dims = (n_dp, n_head, heads, slots, width, latent, share)
+    dma = pltpu.SemaphoreType.DMA
+    query_grad, latent_grad, up_grad = pl.pallas_call(
+        functools.partial(kernel, dims),
+        out_shape=(
+            jax.ShapeDtypeStruct((heads, width, slots), BF16),
+            jax.ShapeDtypeStruct((width, slots), F32),
+            jax.ShapeDtypeStruct((share * heads, vhead), F32),
+        ),
+        in_specs=[pl.BlockSpec(memory_space=pl.ANY)] * 7,
+        out_specs=(
+            pl.BlockSpec(memory_space=pl.ANY),
+            pl.BlockSpec(memory_space=pltpu.VMEM),
+            pl.BlockSpec(memory_space=pltpu.VMEM),
+        ),
+        scratch_shapes=[
+            pltpu.VMEM((heads, width, slots), BF16),
+            pltpu.VMEM((2, width, slots), BF16),
+            pltpu.VMEM((2, 1, slots), jnp.int32),
+            pltpu.VMEM((heads, slots), F32),
+            pltpu.VMEM((slots * heads, latent), BF16),
+            pltpu.VMEM((slots * heads, vhead), BF16),
+            pltpu.VMEM((heads, latent, vhead), BF16),
+            pltpu.VMEM((slots * heads, 128), F32),
+            pltpu.VMEM((slots * heads, 128), F32),
+            pltpu.VMEM((slots * heads, vhead), F32),
+            pltpu.VMEM((heads, slots, latent), BF16),
+            pltpu.VMEM((heads, slots, vhead), BF16),
+            pltpu.VMEM((2 * slots, width), BF16),
+            pltpu.VMEM((width, 2 * slots), BF16),
+            pltpu.VMEM((2 * slots, slots), F32),
+            pltpu.VMEM((2, heads, n_dp, share, vhead), BF16),
+            pltpu.VMEM((heads, n_dp, share, vhead), BF16),
+            pltpu.VMEM((n_dp, heads, share, vhead), BF16),
+            pltpu.VMEM((n_dp, heads, share, vhead), BF16),
+            pltpu.VMEM((piece * n_head, 2 * slots), F32),
+            pltpu.VMEM((n_head, 2, piece, slots), BF16),
+            pltpu.VMEM((n_head, 2, piece, slots), BF16),
+            pltpu.VMEM((2, piece, slots), BF16),
+            pltpu.VMEM((piece, slots), BF16),
+            pltpu.VMEM((n_head, piece, slots), BF16),
+            pltpu.VMEM((heads, width, slots), BF16),
+            dma((7,)),
+            dma((2,)), dma((2,)),
+            dma((CHUNKS,)), dma((CHUNKS,)),
+            dma((n_dp, CHUNKS)), dma((n_dp, CHUNKS)),
+            dma((n_head,)), dma((n_head,)),
+            dma((2,)),
+            dma((n_head,)), dma((n_head,)),
+            dma,
+        ],
+        compiler_params=pltpu.CompilerParams(
+            collective_id=0, has_side_effects=True, vmem_limit_bytes=48 * 1024 * 1024),
+    )(
+        jnp.transpose(queries[0], (1, 2, 0)),
+        latents[0].T,
+        positions,
+        lse[0].T,
+        saved_out.reshape(slots * heads, latent),
+        out_grad.reshape(slots * heads, vhead),
+        value_up,
+    )
+    return (
+        jnp.transpose(query_grad, (2, 0, 1))[None],
+        latent_grad.T[None],
+        up_grad.reshape(share, heads, vhead),
+    )
 
 
 def spans(length):
     return [(lower, min(length, lower + 512)) for lower in range(0, length, 512)]
 
 
-def body(queries, latents, positions, lse, saved_out, out_grad, value_up):
+def spread(queries, latents, positions, lse, saved_out, out_grad, value_up):
     query_rows = queries[0]
     slot_count = query_rows.shape[0]
     head_count = query_rows.shape[1]
@@ -26,11 +339,10 @@
     ).astype(jnp.bfloat16)
     row_delta = jnp.sum(lat_grad.astype(jnp.float32) * saved_out[0].astype(jnp.float32), axis=-1)
     slab_rows = slot_count * lax.axis_size("ctx")
-    grad_init = (
+    carry = (
         jnp.zeros((slot_count, head_count, full_width), jnp.float32),
         jnp.zeros((slab_rows, full_width), jnp.float32),
     )
-    carry = grad_init
     keys_in = lax.all_gather(latents[0], "ctx", axis=0, tiled=True)
     pos_in = lax.all_gather(positions[0], "ctx", axis=0, tiled=True)
     for lower, upper in spans(keys_in.shape[0]):
@@ -73,9 +385,8 @@
     query_acc, key_acc = carry
     summed = lax.psum(key_acc, "head")
     own_rows = lax.psum_scatter(summed, "ctx", scatter_dimension=0, tiled=True)
-    saved_part = saved_out[0]
     weight_share = lax.psum_scatter(
-        jnp.einsum("thl,thv->lhv", saved_part, out_grad[0], preferred_element_type=jnp.float32),
+        jnp.einsum("thl,thv->lhv", saved_out[0], out_grad[0], preferred_element_type=jnp.float32),
         ("dp", "ctx"),
         scatter_dimension=0,
         tiled=True,
@@ -84,6 +395,7 @@
 
 
 def solution(mesh):
+    body = functools.partial(fused, mesh) if mesh.shape["ctx"] == 2 else spread
     return jax.shard_map(
         body,
         mesh=mesh,

time: 134 us -> 39.9 us (0.30)
  waiting for transfers between devices: 82.6 us -> 0 us
  Pallas kernels: 0 us -> 29.5 us
  between operations: 16.9 us -> 0.66 us
  blocking collectives: 10.7 us -> 0 us
  matrix products: 8.16 us -> 0 us
  other arithmetic: 4.24 us -> 0 us
    reduce_scatter x2 -> x0, waiting for transfers between devices: 53.4 us -> none  [the longest x1 39.5 us: body(): lax.psum_scatter(jnp.einsum('thl,thv->lhv', saved_part, out_grad[0], pref...]
    pallas_call x0 -> x1, Pallas kernels: none -> 29.5 us  [fused(): pl.pallas_call(functools.partial(kernel, dims), out_shape=(jax.ShapeDtype...]
    psum x1 -> x0, waiting for transfers between devices: 29.2 us -> none  [body(): summed = lax.psum(key_acc, 'head')]
    all_gather x2 -> x0, blocking collectives: 10.7 us -> none  [the longest x1 5.44 us: body(): pos_in = lax.all_gather(positions[0], 'ctx', axis=0, tiled=True)]
    dot_general x7 -> x0, matrix products: 8.16 us -> none  [the longest x1 2.31 us: update(): jnp.einsum('thd,kd->thk', query_rows, key_rows, preferred_element_type=jn...]
    unnamed x14 -> x17, local copies, waits for them, and re-layouts: 3.29 us -> 9.37 us
    another operation x1 -> x0, local copies, waits for them, and re-layouts: 3.1 us -> none
    reduce_sum x1 -> x0, other arithmetic: 2.21 us -> none  [body(): jnp.sum(lat_grad.astype(jnp.float32) * saved_out[0].astype(jnp.float32),...]
  transfers between devices with their start and end apart: 3 -> 0, of which waited for: 3 -> 0; matrix products, arithmetic and copies ran while one was open for 3% -> 0% of each run, Pallas kernels for 0% -> 0%
where the time goes in v1:
time: 39.9 us; the launch traced here: 39.5 us
  Pallas kernels  29.5 us (74%)
  local copies, waits for them, and re-layouts  9.37 us (23%)
  between operations  0.66 us (2%)
    pallas_call x1, Pallas kernels, fused(): pl.pallas_call(functools.partial(kernel, dims), out_shape=(jax.ShapeDtype...  29.5 us
    unnamed x17, local copies, waits for them, and re-layouts  9.37 us

profile of v1, /device:TPU:0, one launch (start us, length us, event | category | flops | bytes accessed | tf_op | source)
XLA Modules:
  0.0 39.5 jit_solution(7659479093070281697)
XLA Ops:
  0.6 0.0 copy-start
  0.6 1.3 %copy-done = bf16[1,128,16,288]{1,3,2,0:T(8,128)(2,1)S(1)} copy-done((bf16[1,128,16,288]{1,3,2,0:T(8,128)(2,1)S(1)}, bf16[1,128,16,288]{1,3,2,0:T(8,128)(2,1)}, u32[]{:S(2)}) %copy-start) | copy-done | bytes 1179672
  1.9 0.0 copy-start.1
  1.9 1.2 %copy-done.1 = bf16[1,128,16,256]{3,2,1,0:T(8,128)(2,1)S(1)} copy-done((bf16[1,128,16,256]{3,2,1,0:T(8,128)(2,1)S(1)}, bf16[1,128,16,256]{3,2,1,0:T(8,128)(2,1)}, u32[]{:S(2)}) %copy-start.1) | copy-done | bytes 1048600
  3.1 0.0 copy-start.2
  3.1 1.2 %copy-done.2 = bf16[16,256,128]{2,1,0:T(8,128)(2,1)S(1)} copy-done((bf16[16,256,128]{2,1,0:T(8,128)(2,1)S(1)}, bf16[16,256,128]{2,1,0:T(8,128)(2,1)}, u32[]{:S(2)}) %copy-start.2) | copy-done | bytes 1048600
  4.4 0.0 copy-start.3
  4.4 1.0 %copy-done.3 = bf16[1,128,16,128]{3,2,1,0:T(8,128)(2,1)S(1)} copy-done((bf16[1,128,16,128]{3,2,1,0:T(8,128)(2,1)S(1)}, bf16[1,128,16,128]{3,2,1,0:T(8,128)(2,1)}, u32[]{:S(2)}) %copy-start.3) | copy-done | bytes 524312
  5.4 0.0 copy-start.4
  5.4 0.9 %copy-done.4 = bf16[1,128,288]{1,2,0:T(8,128)(2,1)S(1)} copy-done((bf16[1,128,288]{1,2,0:T(8,128)(2,1)S(1)}, bf16[1,128,288]{1,2,0:T(8,128)(2,1)}, u32[]{:S(2)}) %copy-start.4) | copy-done | bytes 73752
  6.3 0.0 copy-start.5
  6.3 0.7 %copy-done.5 = f32[1,128,16]{1,2,0:T(8,128)S(1)} copy-done((f32[1,128,16]{1,2,0:T(8,128)S(1)}, f32[1,128,16]{1,2,0:T(8,128)}, u32[]{:S(2)}) %copy-start.5) | copy-done | bytes 8216
  7.0 0.0 copy-start.6
  7.0 0.7 %copy-done.6 = s32[1,128]{1,0:T(1,128)S(1)} copy-done((s32[1,128]{1,0:T(1,128)S(1)}, s32[1,128]{1,0:T(1,128)}, u32[]{:S(2)}) %copy-start.6) | copy-done | bytes 536
  7.6 29.5 %shard_map.94 = (bf16[16,288,128]{2,1,0:T(8,128)(2,1)S(1)}, f32[288,128]{1,0:T(8,128)S(1)}, f32[512,128]{1,0:T(8,128)S(1)}) custom-call(bf16[16,288,128]{2,1,0:T(8,128)(2,1)S(1)} %bitcast.19, bf16[288,128]{1,0:T(8,128)(2,1)S(1)} %bitcast.24, s32[1,128]{1,0:T(1,128)S(1)} %copy-done.6, f32[16,128]{1,0:T(8,128)S(1)} %bitcast.25, ...), custom_call_target="tpu_custom_call" | custom-call | tf_op jit(solution)/shard_map/pallas_call | solution.py:256
  37.1 1.0 %copy.13 = bf16[1,128,16,288]{1,3,2,0:T(8,128)(2,1)} copy(bf16[1,128,16,288]{1,3,2,0:T(8,128)(2,1)S(1)} %bitcast.18) | data formatting | bytes 2359296
  38.1 0.7 %copy.14 = f32[1,128,288]{1,2,0:T(8,128)} copy(f32[1,128,288]{1,2,0:T(8,128)S(1)} %bitcast.23) | data formatting | bytes 294912
  38.8 0.7 %copy.15 = f32[32,16,128]{2,1,0:T(8,128)} copy(f32[32,16,128]{2,1,0:T(8,128)S(1)} %bitcast.22) | data formatting | bytes 524288
Async XLA Ops:
  0.6 1.3 %copy-start = (bf16[1,128,16,288]{1,3,2,0:T(8,128)(2,1)S(1)}, bf16[1,128,16,288]{1,3,2,0:T(8,128)(2,1)}, u32[]{:S(2)}) copy-start(bf16[1,128,16,288]{1,3,2,0:T(8,128)(2,1)} %param.7) | copy-start | bytes 3538948
  1.9 1.2 %copy-start.1 = (bf16[1,128,16,256]{3,2,1,0:T(8,128)(2,1)S(1)}, bf16[1,128,16,256]{3,2,1,0:T(8,128)(2,1)}, u32[]{:S(2)}) copy-start(bf16[1,128,16,256]{3,2,1,0:T(8,128)(2,1)} %param.11) | copy-start | bytes 3145732
  3.1 1.2 %copy-start.2 = (bf16[16,256,128]{2,1,0:T(8,128)(2,1)S(1)}, bf16[16,256,128]{2,1,0:T(8,128)(2,1)}, u32[]{:S(2)}) copy-start(bf16[16,256,128]{2,1,0:T(8,128)(2,1)} %up_hbm.1) | copy-start | bytes 3145732
  4.4 1.0 %copy-start.3 = (bf16[1,128,16,128]{3,2,1,0:T(8,128)(2,1)S(1)}, bf16[1,128,16,128]{3,2,1,0:T(8,128)(2,1)}, u32[]{:S(2)}) copy-start(bf16[1,128,16,128]{3,2,1,0:T(8,128)(2,1)} %param.12) | copy-start | bytes 1572868
  5.4 0.9 %copy-start.4 = (bf16[1,128,288]{1,2,0:T(8,128)(2,1)S(1)}, bf16[1,128,288]{1,2,0:T(8,128)(2,1)}, u32[]{:S(2)}) copy-start(bf16[1,128,288]{1,2,0:T(8,128)(2,1)} %param.8) | copy-start | bytes 221188
  6.3 0.7 %copy-start.5 = (f32[1,128,16]{1,2,0:T(8,128)S(1)}, f32[1,128,16]{1,2,0:T(8,128)}, u32[]{:S(2)}) copy-start(f32[1,128,16]{1,2,0:T(8,128)} %param.10) | copy-start | bytes 24580
  7.0 0.7 %copy-start.6 = (s32[1,128]{1,0:T(1,128)S(1)}, s32[1,128]{1,0:T(1,128)}, u32[]{:S(2)}) copy-start(s32[1,128]{1,0:T(1,128)} %pos_hbm.1) | copy-start | bytes 1540

commit v2 on v1

--- a/solution.py
+++ b/solution.py
@@ -12,7 +12,7 @@
 MESH = pl.DeviceIdType.MESH
 BF16 = jnp.bfloat16
 F32 = jnp.float32
-CHUNKS = 4
+PER_CHUNK = 2
 
 
 def dot(lhs, rhs, over):
@@ -36,7 +36,7 @@
     scaling = (VHEAD + ROPE) ** -0.5
     my_dp, my_ctx, my_head = lax.axis_index("dp"), lax.axis_index("ctx"), lax.axis_index("head")
     other = 1 - my_ctx
-    per_chunk = heads // CHUNKS
+    chunks = heads // PER_CHUNK
     piece = key_acc.shape[0] // n_head
 
     def load(index, source, target):
@@ -85,28 +85,29 @@
 
     lax.fori_loop(0, 8, widen, 0)
 
-    def up_partial(head, carry):
-        rows = pl.ds(head, slots, heads)
-        low = saved_lo[rows, :].astype(BF16)
-        high = saved_hi[rows, :].astype(BF16)
-        grad = grad_f[rows, :].astype(BF16)
-        saved_h[head, :, :128] = low
-        saved_h[head, :, 128:] = high
-        grad_h[head] = grad
-        product = jnp.concatenate([dot(low, grad, (0, 0)), dot(high, grad, (0, 0))], axis=0).astype(BF16)
-        for dp in range(n_dp):
-            for ctx in range(2):
-                first = (dp * 2 + ctx) * share
-                vx[ctx, head, dp] = product[first:first + share]
+    def x_copy(chunk):
+        part = pl.ds(chunk * PER_CHUNK, PER_CHUNK)
+        return send(vx.at[other, part], vr.at[part], x_send.at[chunk], x_recv.at[chunk], {"ctx": other})
+
+    def up_partial(chunk, carry):
+        for offset in range(PER_CHUNK):
+            head = chunk * PER_CHUNK + offset
+            rows = pl.ds(head, slots, heads)
+            low = saved_lo[rows, :].astype(BF16)
+            high = saved_hi[rows, :].astype(BF16)
+            grad = grad_f[rows, :].astype(BF16)
+            saved_h[head, :, :128] = low
+            saved_h[head, :, 128:] = high
+            grad_h[head] = grad
+            product = jnp.concatenate([dot(low, grad, (0, 0)), dot(high, grad, (0, 0))], axis=0).astype(BF16)
+            for dp in range(n_dp):
+                for ctx in range(2):
+                    first = (dp * 2 + ctx) * share
+                    vx[ctx, head, dp] = product[first:first + share]
+        x_copy(chunk).start()
         return carry
 
-    x_copies = []
-    for chunk in range(CHUNKS):
-        lax.fori_loop(chunk * per_chunk, (chunk + 1) * per_chunk, up_partial, 0)
-        part = pl.ds(chunk * per_chunk, per_chunk)
-        copy = send(vx.at[other, part], vr.at[part], x_send.at[chunk], x_recv.at[chunk], {"ctx": other})
-        copy.start()
-        x_copies.append(copy)
+    lax.fori_loop(0, chunks, up_partial, 0)
 
     lat_copy.wait_recv()
     pos_copy.wait_recv()
@@ -125,7 +126,7 @@
     diagonal = lax.broadcasted_iota(jnp.int32, (slots, slots), 0) == lax.broadcasted_iota(
         jnp.int32, (slots, slots), 1)
 
-    def attend(pair, carry):
+    def attend(pair):
         one, two = 2 * pair, 2 * pair + 1
         lat_grads, deltas = [], []
         for head in (one, two):
@@ -150,34 +151,32 @@
         value_term = dot(lat_grad, weights_b, (1, 1))
         key_acc[:latent, :] += key_term[:latent] + value_term
         key_acc[latent:width, :] += key_term[latent:]
-        return carry
-
-    z_copies = []
+
+    def z_copy(step, chunk, arriving=False):
+        peer = lax.rem(my_dp + step, n_dp)
+        part = pl.ds(chunk * PER_CHUNK, PER_CHUNK)
+        slot = peer if arriving else my_dp
+        return send(zs.at[peer, part], zr.at[slot, part], z_send.at[peer, chunk], z_recv.at[slot, chunk], {"dp": peer})
 
     def forward(chunk):
-        x_copies[chunk].wait_recv()
-
-        def add(head, carry):
+        x_copy(chunk).wait_recv()
+        for offset in range(PER_CHUNK):
+            head = chunk * PER_CHUNK + offset
             for dp in range(n_dp):
                 zs[dp, head] = (vx[my_ctx, head, dp].astype(F32) + vr[head, dp].astype(F32)).astype(BF16)
-            return carry
-
-        lax.fori_loop(chunk * per_chunk, (chunk + 1) * per_chunk, add, 0)
-        part = pl.ds(chunk * per_chunk, per_chunk)
         for step in range(1, n_dp):
-            to = lax.rem(my_dp + step, n_dp)
-            copy = send(zs.at[to, part], zr.at[my_dp, part], z_send.at[to, chunk], z_recv.at[my_dp, chunk], {"dp": to})
-            copy.start()
-            z_copies.append(copy)
-
-    def attend_chunk(chunk):
-        lax.fori_loop(chunk * per_chunk // 2, (chunk + 1) * per_chunk // 2, attend, 0)
-
-    attend_chunk(0)
-    attend_chunk(1)
-    forward(0)
-    attend_chunk(2)
-    attend_chunk(3)
+            z_copy(step, chunk).start()
+
+    def attend_and_forward(pair, carry):
+        attend(pair)
+
+        @pl.when(pair >= 1)
+        def _():
+            forward(pair - 1)
+
+        return carry
+
+    lax.fori_loop(0, chunks, attend_and_forward, 0)
     qg_copy = pltpu.make_async_copy(qg_ref, qg_hbm, out_sem)
     qg_copy.start()
 
@@ -192,7 +191,7 @@
         copy.start()
         ka_copies.append(copy)
 
-    forward(1)
+    forward(chunks - 1)
 
     sums = ka_send[my_head].astype(F32)
     for step in range(1, n_head):
@@ -203,8 +202,6 @@
     kb_copy = send(kb_send.at[other], kb_recv, kb_sem.at[0], kb_sem.at[1], {"ctx": other})
     kb_copy.start()
 
-    forward(2)
-
     kb_copy.wait_recv()
     kc[my_head] = (kb_send[my_ctx].astype(F32) + kb_recv[...].astype(F32)).astype(BF16)
     kc_copies = []
@@ -214,8 +211,6 @@
         copy.start()
         kc_copies.append(copy)
 
-    forward(3)
-
     for step in range(1, n_head):
         src = lax.rem(my_head + step, n_head)
         send(kc.at[src], kc.at[src], kc_ssem.at[src], kc_rsem.at[src], {"head": src}).wait_recv()
@@ -223,24 +218,39 @@
         first, last = part * piece, min((part + 1) * piece, width)
         lg_out[first:last, :] = kc[part, :last - first, :].astype(F32)
 
-    def finish(head, carry):
-        total = zs[my_dp, head].astype(F32)
+    def finish(chunk, carry):
         for step in range(1, n_dp):
-            total = total + zr[lax.rem(my_dp + step, n_dp), head].astype(F32)
-        vg_out[pl.ds(head, share, heads), :] = total
+            z_copy(step, chunk, arriving=True).wait_recv()
+        for offset in range(PER_CHUNK):
+            head = chunk * PER_CHUNK + offset
+            total = zs[my_dp, head].astype(F32)
+            for step in range(1, n_dp):
+                total = total + zr[lax.rem(my_dp + step, n_dp), head].astype(F32)
+            vg_out[pl.ds(head, share, heads), :] = total
         return carry
 
-    for chunk in range(CHUNKS):
-        part = pl.ds(chunk * per_chunk, per_chunk)
+    lax.fori_loop(0, chunks, finish, 0)
+
+    def drain(chunk, carry):
+        x_copy(chunk).wait_send()
         for step in range(1, n_dp):
-            src = lax.rem(my_dp + step, n_dp)
-            send(zs.at[src, part], zr.at[src, part], z_send.at[src, chunk], z_recv.at[src, chunk],
-                 {"dp": src}).wait_recv()
-        lax.fori_loop(chunk * per_chunk, (chunk + 1) * per_chunk, finish, 0)
-
-    for copy in [lat_copy, pos_copy, kb_copy] + x_copies + z_copies + ka_copies + kc_copies:
+            z_copy(step, chunk).wait_send()
+        return carry
+
+    lax.fori_loop(0, chunks, drain, 0)
+    for copy in [lat_copy, pos_copy, kb_copy] + ka_copies + kc_copies:
         copy.wait_send()
     qg_copy.wait()
+
+
+def write_out(*refs):
+    count = len(refs) // 2
+    sems = refs[-1]
+    copies = [pltpu.make_async_copy(refs[i], refs[count + i], sems.at[i]) for i in range(count)]
+    for copy in copies:
+        copy.start()
+    for copy in copies:
+        copy.wait()
 
 
 def fused(mesh, queries, latents, positions, lse, saved_out, out_grad, value_up):
@@ -253,14 +263,15 @@
     piece = -(-width // unit) * 16
     dims = (n_dp, n_head, heads, slots, width, latent, share)
     dma = pltpu.SemaphoreType.DMA
-    query_grad, latent_grad, up_grad = pl.pallas_call(
+    chunks = heads // PER_CHUNK
+    results = pl.pallas_call(
         functools.partial(kernel, dims),
         out_shape=(
             jax.ShapeDtypeStruct((heads, width, slots), BF16),
             jax.ShapeDtypeStruct((width, slots), F32),
             jax.ShapeDtypeStruct((share * heads, vhead), F32),
         ),
-        in_specs=[pl.BlockSpec(memory_space=pl.ANY)] * 7,
+        in_specs=[pl.BlockSpec(memory_space=pltpu.HBM)] * 7,
         out_specs=(
             pl.BlockSpec(memory_space=pl.ANY),
             pl.BlockSpec(memory_space=pltpu.VMEM),
@@ -295,15 +306,15 @@
             pltpu.VMEM((heads, width, slots), BF16),
             dma((7,)),
             dma((2,)), dma((2,)),
-            dma((CHUNKS,)), dma((CHUNKS,)),
-            dma((n_dp, CHUNKS)), dma((n_dp, CHUNKS)),
+            dma((chunks,)), dma((chunks,)),
+            dma((n_dp, chunks)), dma((n_dp, chunks)),
             dma((n_head,)), dma((n_head,)),
             dma((2,)),
             dma((n_head,)), dma((n_head,)),
             dma,
         ],
         compiler_params=pltpu.CompilerParams(
-            collective_id=0, has_side_effects=True, vmem_limit_bytes=48 * 1024 * 1024),
+            collective_id=0, has_side_effects=True, vmem_limit_bytes=64 * 1024 * 1024),
     )(
         jnp.transpose(queries[0], (1, 2, 0)),
         latents[0].T,
@@ -313,6 +324,14 @@
         out_grad.reshape(slots * heads, vhead),
         value_up,
     )
+    query_grad, latent_grad, up_grad = pl.pallas_call(
+        write_out,
+        out_shape=tuple(jax.ShapeDtypeStruct(r.shape, r.dtype) for r in results),
+        in_specs=[pl.BlockSpec(memory_space=pl.ANY)] * 3,
+        out_specs=(pl.BlockSpec(memory_space=pl.ANY),) * 3,
+        scratch_shapes=[dma((3,))],
+        compiler_params=pltpu.CompilerParams(vmem_limit_bytes=64 * 1024 * 1024),
+    )(*results)
     return (
         jnp.transpose(query_grad, (2, 0, 1))[None],
         latent_grad.T[None],

time: 39.9 us -> 79.7 us (2.00)
  Pallas kernels: 29.5 us -> 78.9 us
  local copies, waits for them, and re-layouts: 9.37 us -> 0 us
    pallas_call x0 -> x1, Pallas kernels: none -> 49.3 us  [fused(): pl.pallas_call(write_out, out_shape=tuple((jax.ShapeDtypeStruct(r.shape,...]
    unnamed x17 -> x0, local copies, waits for them, and re-layouts: 9.37 us -> none
where the time goes in v2:
time: 79.7 us; the launch traced here: 79.5 us
  Pallas kernels  78.9 us (99%)
    pallas_call x1, Pallas kernels, fused(): pl.pallas_call(write_out, out_shape=tuple((jax.ShapeDtypeStruct(r.shape,...  49.3 us
    pallas_call x1, Pallas kernels, fused(): pl.pallas_call(functools.partial(kernel, dims), out_shape=(jax.ShapeDtype...  29.6 us

profile of v2, /device:TPU:0, one launch (start us, length us, event | category | flops | bytes accessed | tf_op | source)
XLA Modules:
  0.0 79.5 jit_solution(17189246656186561656)
XLA Ops:
  0.6 29.6 %shard_map.94 = (bf16[16,288,128]{2,1,0:T(8,128)(2,1)}, f32[288,128]{1,0:T(8,128)}, f32[512,128]{1,0:T(8,128)}) custom-call(bf16[16,288,128]{2,1,0:T(8,128)(2,1)} %bitcast.18, bf16[288,128]{1,0:T(8,128)(2,1)} %bitcast.21, s32[1,128]{1,0:T(1,128)} %pos_hbm.1, f32[16,128]{1,0:T(8,128)} %bitcast.22, bf16[2048,256]{1,0:T(8,128)(2,1)} %bitcast.19, ...), custom_call_target="tpu_custom_call" | custom-call | tf_op jit(solution)/shard_map/pallas_call | solution.py:267
  30.2 49.3 %shard_map.95 = (bf16[16,288,128]{2,1,0:T(8,128)(2,1)}, f32[288,128]{1,0:T(8,128)}, f32[512,128]{1,0:T(8,128)}) custom-call(bf16[16,288,128]{2,1,0:T(8,128)(2,1)} %get-tuple-element.9.refs_0_, f32[288,128]{1,0:T(8,128)} %get-tuple-element.10.refs_1_, f32[512,128]{1,0:T(8,128)} %get-tuple-element.11.refs_2_), custom_call_target="tpu_custom_call" | custom-call | tf_op jit(solution)/shard_map/pallas_call | solution.py:327

commit v3 on v2

--- a/solution.py
+++ b/solution.py
@@ -12,11 +12,17 @@
 MESH = pl.DeviceIdType.MESH
 BF16 = jnp.bfloat16
 F32 = jnp.float32
-PER_CHUNK = 2
+PER_CHUNK = 4
 
 
 def dot(lhs, rhs, over):
     return lax.dot_general(lhs, rhs, (((over[0],), (over[1],)), ((), ())), preferred_element_type=F32)
+
+
+def slab_peers(my_ctx, my_head, n_head):
+    ahead = [{"ctx": my_ctx, "head": lax.rem(my_head + step, n_head)} for step in range(1, n_head)]
+    across = [{"ctx": 1 - my_ctx, "head": lax.rem(my_head + step, n_head)} for step in range(n_head)]
+    return across + ahead
 
 
 def kernel(
@@ -24,13 +30,13 @@
     q_hbm, lat_hbm, pos_hbm, lse_hbm, saved_hbm, grad_hbm, up_hbm,
     qg_hbm, lg_out, vg_out,
     q_ref, kt_in, pos_in, lse_ref, saved_b, grad_b, up_ref,
-    saved_lo, saved_hi, grad_f, saved_h, grad_h,
+    saved_lo, saved_hi, grad_f, lat_grads, deltas, dlogits_all,
     keys, keys_t, bias,
     vx, vr, zs, zr,
-    key_acc, ka_send, ka_recv, kb_send, kb_recv, kc,
+    key_acc, ka_send, ka_recv, kc,
     qg_ref,
     in_sem, lat_send, lat_recv, x_send, x_recv, z_send, z_recv,
-    ka_ssem, ka_rsem, kb_sem, kc_ssem, kc_rsem, out_sem,
+    ka_ssem, ka_rsem, kc_ssem, kc_rsem, out_sem,
 ):
     n_dp, n_head, heads, slots, width, latent, share = dims
     scaling = (VHEAD + ROPE) ** -0.5
@@ -53,14 +59,13 @@
     lse_in = load(6, lse_hbm, lse_ref)
 
     barrier = pltpu.get_barrier_semaphore()
-    pl.semaphore_signal(barrier, inc=1, device_id={"ctx": other}, device_id_type=MESH)
     for step in range(1, n_dp):
         pl.semaphore_signal(barrier, inc=1, device_id={"dp": lax.rem(my_dp + step, n_dp)}, device_id_type=MESH)
-    for step in range(1, n_head):
-        pl.semaphore_signal(barrier, inc=1, device_id={"head": lax.rem(my_head + step, n_head)}, device_id_type=MESH)
+    for where in slab_peers(my_ctx, my_head, n_head):
+        pl.semaphore_signal(barrier, inc=1, device_id=where, device_id_type=MESH)
     lat_in.wait()
     pos_load.wait()
-    pl.semaphore_wait(barrier, 1 + (n_dp - 1) + (n_head - 1))
+    pl.semaphore_wait(barrier, (n_dp - 1) + (2 * n_head - 1))
 
     def send(source, target, send_sem, recv_sem, where):
         return pltpu.make_async_remote_copy(
@@ -89,22 +94,32 @@
         part = pl.ds(chunk * PER_CHUNK, PER_CHUNK)
         return send(vx.at[other, part], vr.at[part], x_send.at[chunk], x_recv.at[chunk], {"ctx": other})
 
+    diagonal = lax.broadcasted_iota(jnp.int32, (slots, slots), 0) == lax.broadcasted_iota(
+        jnp.int32, (slots, slots), 1)
+    up_in.wait()
+
     def up_partial(chunk, carry):
-        for offset in range(PER_CHUNK):
-            head = chunk * PER_CHUNK + offset
+        members = [chunk * PER_CHUNK + offset for offset in range(PER_CHUNK)]
+        lows, highs, grads = [], [], []
+        for head in members:
             rows = pl.ds(head, slots, heads)
-            low = saved_lo[rows, :].astype(BF16)
-            high = saved_hi[rows, :].astype(BF16)
-            grad = grad_f[rows, :].astype(BF16)
-            saved_h[head, :, :128] = low
-            saved_h[head, :, 128:] = high
-            grad_h[head] = grad
+            lows.append(saved_lo[rows, :].astype(BF16))
+            highs.append(saved_hi[rows, :].astype(BF16))
+            grads.append(grad_f[rows, :].astype(BF16))
+        for head, low, high, grad in zip(members, lows, highs, grads):
             product = jnp.concatenate([dot(low, grad, (0, 0)), dot(high, grad, (0, 0))], axis=0).astype(BF16)
             for dp in range(n_dp):
                 for ctx in range(2):
                     first = (dp * 2 + ctx) * share
                     vx[ctx, head, dp] = product[first:first + share]
         x_copy(chunk).start()
+        raised = [dot(up_ref[head], grad, (1, 1)).astype(BF16) for head, grad in zip(members, grads)]
+        lat_grads[chunk] = jnp.concatenate(raised, axis=1)
+        sums = []
+        for low, high, lat_grad in zip(lows, highs, raised):
+            full = dot(jnp.concatenate([low, high], axis=1), lat_grad, (1, 0))
+            sums.append(jnp.sum(jnp.where(diagonal, full, 0.0), axis=0, keepdims=True))
+        deltas[chunk] = jnp.concatenate(sums, axis=1)
         return carry
 
     lax.fori_loop(0, chunks, up_partial, 0)
@@ -120,35 +135,22 @@
         key_pos = jnp.broadcast_to(pos_in[half], (slots, slots)).T
         bias[cols, :] = jnp.where(key_pos <= query_pos, 0.0, -1e30)
     key_acc[...] = jnp.zeros_like(key_acc)
-    up_in.wait()
     q_in.wait()
     lse_in.wait()
-    diagonal = lax.broadcasted_iota(jnp.int32, (slots, slots), 0) == lax.broadcasted_iota(
-        jnp.int32, (slots, slots), 1)
-
-    def attend(pair):
-        one, two = 2 * pair, 2 * pair + 1
-        lat_grads, deltas = [], []
-        for head in (one, two):
-            lat_grad = dot(up_ref[head], grad_h[head], (1, 1)).astype(BF16)
-            lat_grads.append(lat_grad)
-            full = dot(saved_h[head], lat_grad, (1, 0))
-            deltas.append(jnp.sum(jnp.where(diagonal, full, 0.0), axis=0, keepdims=True))
-        lat_grad = jnp.concatenate(lat_grads, axis=1)
-        delta = jnp.concatenate(deltas, axis=1)
-        query = jnp.concatenate([q_ref[one], q_ref[two]], axis=1)
-        lse = jnp.concatenate([lse_ref[pl.ds(one, 1), :], lse_ref[pl.ds(two, 1), :]], axis=1)
-        mask = jnp.concatenate([bias[...], bias[...]], axis=1)
+
+    def attend(chunk):
+        members = [chunk * PER_CHUNK + offset for offset in range(PER_CHUNK)]
+        query = jnp.concatenate([q_ref[head] for head in members], axis=1)
+        lse = jnp.concatenate([lse_ref[pl.ds(head, 1), :] for head in members], axis=1)
+        mask = jnp.concatenate([bias[...]] * PER_CHUNK, axis=1)
+        lat_grad = lat_grads[chunk]
         logits = dot(keys[...], query, (1, 0)) * scaling
+        dot_value = dot(keys[:, :latent], lat_grad, (1, 0))
         weights = jnp.exp(logits - lse + mask)
-        dot_value = dot(keys[:, :latent], lat_grad, (1, 0))
-        dlogits = (weights * (dot_value - delta) * scaling).astype(BF16)
-        weights_b = weights.astype(BF16)
-        query_grad = dot(keys_t[...], dlogits, (1, 0)).astype(BF16)
-        qg_ref[one] = query_grad[:, :slots]
-        qg_ref[two] = query_grad[:, slots:]
+        dlogits = (weights * (dot_value - deltas[chunk]) * scaling).astype(BF16)
+        dlogits_all[chunk] = dlogits
         key_term = dot(query, dlogits, (1, 1))
-        value_term = dot(lat_grad, weights_b, (1, 1))
+        value_term = dot(lat_grad, weights.astype(BF16), (1, 1))
         key_acc[:latent, :] += key_term[:latent] + value_term
         key_acc[latent:width, :] += key_term[latent:]
 
@@ -167,56 +169,54 @@
         for step in range(1, n_dp):
             z_copy(step, chunk).start()
 
-    def attend_and_forward(pair, carry):
-        attend(pair)
-
-        @pl.when(pair >= 1)
+    def attend_and_forward(chunk, carry):
+        attend(chunk)
+
+        @pl.when(chunk < chunks - 1)
         def _():
-            forward(pair - 1)
+            forward(chunk)
 
         return carry
 
     lax.fori_loop(0, chunks, attend_and_forward, 0)
+
+    for ctx in range(2):
+        for part in range(n_head):
+            ka_send[ctx, part] = key_acc[
+                part * piece:(part + 1) * piece, ctx * slots:(ctx + 1) * slots].astype(BF16)
+
+    def ka_copy(where, arriving=False):
+        theirs, mine = (where["ctx"], where["head"]), (my_ctx, my_head)
+        slot = theirs if arriving else mine
+        return send(ka_send.at[theirs], ka_recv.at[slot], ka_ssem.at[theirs], ka_rsem.at[slot], where)
+
+    peers = slab_peers(my_ctx, my_head, n_head)
+    for where in peers:
+        ka_copy(where).start()
+
+    forward(chunks - 1)
+
+    def query_grads(chunk, carry):
+        query_grad = dot(keys_t[...], dlogits_all[chunk], (1, 0)).astype(BF16)
+        for offset in range(PER_CHUNK):
+            qg_ref[chunk * PER_CHUNK + offset] = query_grad[:, offset * slots:(offset + 1) * slots]
+        return carry
+
+    lax.fori_loop(0, chunks, query_grads, 0)
     qg_copy = pltpu.make_async_copy(qg_ref, qg_hbm, out_sem)
     qg_copy.start()
 
-    for part in range(n_head):
-        for ctx in range(2):
-            ka_send[part, ctx] = key_acc[
-                part * piece:(part + 1) * piece, ctx * slots:(ctx + 1) * slots].astype(BF16)
-    ka_copies = []
-    for step in range(1, n_head):
-        to = lax.rem(my_head + step, n_head)
-        copy = send(ka_send.at[to], ka_recv.at[my_head], ka_ssem.at[to], ka_rsem.at[my_head], {"head": to})
-        copy.start()
-        ka_copies.append(copy)
-
-    forward(chunks - 1)
-
-    sums = ka_send[my_head].astype(F32)
-    for step in range(1, n_head):
-        src = lax.rem(my_head + step, n_head)
-        send(ka_send.at[src], ka_recv.at[src], ka_ssem.at[src], ka_rsem.at[src], {"head": src}).wait_recv()
-        sums = sums + ka_recv[src].astype(F32)
-    kb_send[...] = sums.astype(BF16)
-    kb_copy = send(kb_send.at[other], kb_recv, kb_sem.at[0], kb_sem.at[1], {"ctx": other})
-    kb_copy.start()
-
-    kb_copy.wait_recv()
-    kc[my_head] = (kb_send[my_ctx].astype(F32) + kb_recv[...].astype(F32)).astype(BF16)
+    sums = ka_send[my_ctx, my_head].astype(F32)
+    for where in peers:
+        ka_copy(where, arriving=True).wait_recv()
+        sums = sums + ka_recv[where["ctx"], where["head"]].astype(F32)
+    kc[my_head] = sums.astype(BF16)
     kc_copies = []
     for step in range(1, n_head):
         to = lax.rem(my_head + step, n_head)
         copy = send(kc.at[my_head], kc.at[my_head], kc_ssem.at[to], kc_rsem.at[my_head], {"head": to})
         copy.start()
         kc_copies.append(copy)
-
-    for step in range(1, n_head):
-        src = lax.rem(my_head + step, n_head)
-        send(kc.at[src], kc.at[src], kc_ssem.at[src], kc_rsem.at[src], {"head": src}).wait_recv()
-    for part in range(n_head):
-        first, last = part * piece, min((part + 1) * piece, width)
-        lg_out[first:last, :] = kc[part, :last - first, :].astype(F32)
 
     def finish(chunk, carry):
         for step in range(1, n_dp):
@@ -231,6 +231,13 @@
 
     lax.fori_loop(0, chunks, finish, 0)
 
+    for step in range(1, n_head):
+        src = lax.rem(my_head + step, n_head)
+        send(kc.at[src], kc.at[src], kc_ssem.at[src], kc_rsem.at[src], {"head": src}).wait_recv()
+    for part in range(n_head):
+        first, last = part * piece, min((part + 1) * piece, width)
+        lg_out[first:last, :] = kc[part, :last - first, :].astype(F32)
+
     def drain(chunk, carry):
         x_copy(chunk).wait_send()
         for step in range(1, n_dp):
@@ -238,19 +245,30 @@
         return carry
 
     lax.fori_loop(0, chunks, drain, 0)
-    for copy in [lat_copy, pos_copy, kb_copy] + ka_copies + kc_copies:
+    for copy in [lat_copy, pos_copy] + [ka_copy(where) for where in peers] + kc_copies:
         copy.wait_send()
     qg_copy.wait()
 
 
 def write_out(*refs):
-    count = len(refs) // 2
-    sems = refs[-1]
-    copies = [pltpu.make_async_copy(refs[i], refs[count + i], sems.at[i]) for i in range(count)]
-    for copy in copies:
-        copy.start()
-    for copy in copies:
-        copy.wait()
+    sources, targets, rooms, (in_sem, out_sem) = refs[:3], refs[3:6], refs[6:9], refs[9:]
+    pieces = []
+    for source, target, room in zip(sources, targets, rooms):
+        count = 4 if source.ndim == 3 else 1
+        size = source.shape[0] // count
+        for part in range(count):
+            rows = pl.ds(part * size, size)
+            index = len(pieces)
+            pieces.append((
+                pltpu.make_async_copy(source.at[rows], room.at[rows], in_sem.at[index]),
+                pltpu.make_async_copy(room.at[rows], target.at[rows], out_sem.at[index])))
+    for come, _ in pieces:
+        come.start()
+    for come, leave in pieces:
+        come.wait()
+        leave.start()
+    for _, leave in pieces:
+        leave.wait()
 
 
 def fused(mesh, queries, latents, positions, lse, saved_out, out_grad, value_up):
@@ -288,8 +306,9 @@
             pltpu.VMEM((slots * heads, 128), F32),
             pltpu.VMEM((slots * heads, 128), F32),
             pltpu.VMEM((slots * heads, vhead), F32),
-            pltpu.VMEM((heads, slots, latent), BF16),
-            pltpu.VMEM((heads, slots, vhead), BF16),
+            pltpu.VMEM((chunks, latent, PER_CHUNK * slots), BF16),
+            pltpu.VMEM((chunks, 1, PER_CHUNK * slots), F32),
+            pltpu.VMEM((chunks, 2 * slots, PER_CHUNK * slots), BF16),
             pltpu.VMEM((2 * slots, width), BF16),
             pltpu.VMEM((width, 2 * slots), BF16),
             pltpu.VMEM((2 * slots, slots), F32),
@@ -298,18 +317,15 @@
             pltpu.VMEM((n_dp, heads, share, vhead), BF16),
             pltpu.VMEM((n_dp, heads, share, vhead), BF16),
             pltpu.VMEM((piece * n_head, 2 * slots), F32),
-            pltpu.VMEM((n_head, 2, piece, slots), BF16),
-            pltpu.VMEM((n_head, 2, piece, slots), BF16),
-            pltpu.VMEM((2, piece, slots), BF16),
-            pltpu.VMEM((piece, slots), BF16),
+            pltpu.VMEM((2, n_head, piece, slots), BF16),
+            pltpu.VMEM((2, n_head, piece, slots), BF16),
             pltpu.VMEM((n_head, piece, slots), BF16),
             pltpu.VMEM((heads, width, slots), BF16),
             dma((7,)),
             dma((2,)), dma((2,)),
             dma((chunks,)), dma((chunks,)),
             dma((n_dp, chunks)), dma((n_dp, chunks)),
-            dma((n_head,)), dma((n_head,)),
-            dma((2,)),
+            dma((2, n_head)), dma((2, n_head)),
             dma((n_head,)), dma((n_head,)),
             dma,
         ],
@@ -329,7 +345,7 @@
         out_shape=tuple(jax.ShapeDtypeStruct(r.shape, r.dtype) for r in results),
         in_specs=[pl.BlockSpec(memory_space=pl.ANY)] * 3,
         out_specs=(pl.BlockSpec(memory_space=pl.ANY),) * 3,
-        scratch_shapes=[dma((3,))],
+        scratch_shapes=[pltpu.VMEM(r.shape, r.dtype) for r in results] + [dma((6,)), dma((6,))],
         compiler_params=pltpu.CompilerParams(vmem_limit_bytes=64 * 1024 * 1024),
     )(*results)
     return (

time: 79.7 us -> 29.5 us (0.37)
  Pallas kernels: 78.9 us -> 28.8 us
    pallas_call x1, Pallas kernels: 49.3 us -> 2.21 us  [fused(): pl.pallas_call(write_out, out_shape=tuple((jax.ShapeDtypeStruct(r.shape,...]
    pallas_call x1, Pallas kernels: 29.6 us -> 26.5 us  [fused(): pl.pallas_call(functools.partial(kernel, dims), out_shape=(jax.ShapeDtype...]
where the time goes in v3:
time: 29.5 us; the launch traced here: 29.4 us
  Pallas kernels  28.8 us (98%)
  between operations  0.64 us (2%)
    pallas_call x1, Pallas kernels, fused(): pl.pallas_call(functools.partial(kernel, dims), out_shape=(jax.ShapeDtype...  26.5 us
    pallas_call x1, Pallas kernels, fused(): pl.pallas_call(write_out, out_shape=tuple((jax.ShapeDtypeStruct(r.shape,...  2.21 us

profile of v3, /device:TPU:0, one launch (start us, length us, event | category | flops | bytes accessed | tf_op | source)
XLA Modules:
  0.0 29.4 jit_solution(16084519931081936992)
XLA Ops:
  0.6 26.5 %shard_map.94 = (bf16[16,288,128]{2,1,0:T(8,128)(2,1)}, f32[288,128]{1,0:T(8,128)}, f32[512,128]{1,0:T(8,128)}) custom-call(bf16[16,288,128]{2,1,0:T(8,128)(2,1)} %bitcast.18, bf16[288,128]{1,0:T(8,128)(2,1)} %bitcast.21, s32[1,128]{1,0:T(1,128)} %pos_hbm.1, f32[16,128]{1,0:T(8,128)} %bitcast.22, bf16[2048,256]{1,0:T(8,128)(2,1)} %bitcast.19, ...), custom_call_target="tpu_custom_call" | custom-call | tf_op jit(solution)/shard_map/pallas_call | solution.py:285
  27.2 2.2 %shard_map.95 = (bf16[16,288,128]{2,1,0:T(8,128)(2,1)}, f32[288,128]{1,0:T(8,128)}, f32[512,128]{1,0:T(8,128)}) custom-call(bf16[16,288,128]{2,1,0:T(8,128)(2,1)} %get-tuple-element.9.refs_0_, f32[288,128]{1,0:T(8,128)} %get-tuple-element.10.refs_1_, f32[512,128]{1,0:T(8,128)} %get-tuple-element.11.refs_2_), custom_call_target="tpu_custom_call" | custom-call | tf_op jit(solution)/shard_map/pallas_call | solution.py:343

commit v4 on v2

--- a/solution.py
+++ b/solution.py
@@ -13,6 +13,7 @@
 BF16 = jnp.bfloat16
 F32 = jnp.float32
 PER_CHUNK = 2
+PER_STEP = 4
 
 
 def dot(lhs, rhs, over):
@@ -22,21 +23,21 @@
 def kernel(
     dims,
     q_hbm, lat_hbm, pos_hbm, lse_hbm, saved_hbm, grad_hbm, up_hbm,
-    qg_hbm, lg_out, vg_out,
+    qg_hbm, lg_hbm, vg_hbm,
     q_ref, kt_in, pos_in, lse_ref, saved_b, grad_b, up_ref,
-    saved_lo, saved_hi, grad_f, saved_h, grad_h,
+    saved_lo, saved_hi, grad_f, saved_h, grad_h, lat_grads, deltas, dlogits_all,
     keys, keys_t, bias,
     vx, vr, zs, zr,
     key_acc, ka_send, ka_recv, kb_send, kb_recv, kc,
-    qg_ref,
+    qg_ref, lg_ref, vg_ref,
     in_sem, lat_send, lat_recv, x_send, x_recv, z_send, z_recv,
-    ka_ssem, ka_rsem, kb_sem, kc_ssem, kc_rsem, out_sem,
+    ka_ssem, ka_rsem, kb_sem, kc_ssem, kc_rsem, out_sem, vg_sem,
 ):
     n_dp, n_head, heads, slots, width, latent, share = dims
     scaling = (VHEAD + ROPE) ** -0.5
     my_dp, my_ctx, my_head = lax.axis_index("dp"), lax.axis_index("ctx"), lax.axis_index("head")
     other = 1 - my_ctx
-    chunks = heads // PER_CHUNK
+    chunks, steps, ratio = heads // PER_CHUNK, heads // PER_STEP, PER_STEP // PER_CHUNK
     piece = key_acc.shape[0] // n_head
 
     def load(index, source, target):
@@ -48,32 +49,24 @@
     pos_load = load(1, pos_hbm, pos_in.at[my_ctx])
     saved_in = load(2, saved_hbm, saved_b)
     grad_in = load(3, grad_hbm, grad_b)
-    up_in = load(4, up_hbm, up_ref)
-    q_in = load(5, q_hbm, q_ref)
-    lse_in = load(6, lse_hbm, lse_ref)
 
     barrier = pltpu.get_barrier_semaphore()
-    pl.semaphore_signal(barrier, inc=1, device_id={"ctx": other}, device_id_type=MESH)
     for step in range(1, n_dp):
         pl.semaphore_signal(barrier, inc=1, device_id={"dp": lax.rem(my_dp + step, n_dp)}, device_id_type=MESH)
     for step in range(1, n_head):
         pl.semaphore_signal(barrier, inc=1, device_id={"head": lax.rem(my_head + step, n_head)}, device_id_type=MESH)
-    lat_in.wait()
-    pos_load.wait()
-    pl.semaphore_wait(barrier, 1 + (n_dp - 1) + (n_head - 1))
+    pl.semaphore_signal(barrier, inc=1, device_id={"ctx": other}, device_id_type=MESH)
 
     def send(source, target, send_sem, recv_sem, where):
         return pltpu.make_async_remote_copy(
             src_ref=source, dst_ref=target, send_sem=send_sem, recv_sem=recv_sem,
             device_id=where, device_id_type=MESH)
 
-    lat_copy = send(kt_in.at[my_ctx], kt_in.at[my_ctx], lat_send.at[0], lat_recv.at[0], {"ctx": other})
-    pos_copy = send(pos_in.at[my_ctx], pos_in.at[my_ctx], lat_send.at[1], lat_recv.at[1], {"ctx": other})
-    lat_copy.start()
-    pos_copy.start()
-
     saved_in.wait()
     grad_in.wait()
+    up_in = load(4, up_hbm, up_ref)
+    q_in = load(5, q_hbm, q_ref)
+    lse_in = load(6, lse_hbm, lse_ref)
     rows_step = (slots * heads) // 8
 
     def widen(step, carry):
@@ -85,29 +78,56 @@
 
     lax.fori_loop(0, 8, widen, 0)
 
+    lat_in.wait()
+    pos_load.wait()
+    pl.semaphore_wait(barrier, (n_dp - 1) + (n_head - 1) + 1)
+    lat_copy = send(kt_in.at[my_ctx], kt_in.at[my_ctx], lat_send.at[0], lat_recv.at[0], {"ctx": other})
+    pos_copy = send(pos_in.at[my_ctx], pos_in.at[my_ctx], lat_send.at[1], lat_recv.at[1], {"ctx": other})
+    lat_copy.start()
+    pos_copy.start()
+
     def x_copy(chunk):
         part = pl.ds(chunk * PER_CHUNK, PER_CHUNK)
         return send(vx.at[other, part], vr.at[part], x_send.at[chunk], x_recv.at[chunk], {"ctx": other})
 
-    def up_partial(chunk, carry):
-        for offset in range(PER_CHUNK):
-            head = chunk * PER_CHUNK + offset
-            rows = pl.ds(head, slots, heads)
-            low = saved_lo[rows, :].astype(BF16)
-            high = saved_hi[rows, :].astype(BF16)
-            grad = grad_f[rows, :].astype(BF16)
-            saved_h[head, :, :128] = low
-            saved_h[head, :, 128:] = high
-            grad_h[head] = grad
-            product = jnp.concatenate([dot(low, grad, (0, 0)), dot(high, grad, (0, 0))], axis=0).astype(BF16)
-            for dp in range(n_dp):
-                for ctx in range(2):
-                    first = (dp * 2 + ctx) * share
-                    vx[ctx, head, dp] = product[first:first + share]
-        x_copy(chunk).start()
-        return carry
-
-    lax.fori_loop(0, chunks, up_partial, 0)
+    def up_partial(step, carry):
+        for part in range(ratio):
+            chunk = step * ratio + part
+            for offset in range(PER_CHUNK):
+                head = chunk * PER_CHUNK + offset
+                rows = pl.ds(head, slots, heads)
+                low = saved_lo[rows, :].astype(BF16)
+                high = saved_hi[rows, :].astype(BF16)
+                grad = grad_f[rows, :].astype(BF16)
+                saved_h[head, :, :128] = low
+                saved_h[head, :, 128:] = high
+                grad_h[head] = grad
+                product = jnp.concatenate([dot(low, grad, (0, 0)), dot(high, grad, (0, 0))], axis=0).astype(BF16)
+                for dp in range(n_dp):
+                    for ctx in range(2):
+                        first = (dp * 2 + ctx) * share
+                        vx[ctx, head, dp] = product[first:first + share]
+            x_copy(chunk).start()
+        return carry
+
+    lax.fori_loop(0, steps, up_partial, 0)
+
+    diagonal = lax.broadcasted_iota(jnp.int32, (slots, slots), 0) == lax.broadcasted_iota(
+        jnp.int32, (slots, slots), 1)
+    up_in.wait()
+
+    def raise_grads(step, carry):
+        members = [step * PER_STEP + offset for offset in range(PER_STEP)]
+        raised = [dot(up_ref[head], grad_h[head], (1, 1)).astype(BF16) for head in members]
+        lat_grads[step] = jnp.concatenate(raised, axis=1)
+        sums = []
+        for head, lat_grad in zip(members, raised):
+            full = dot(saved_h[head], lat_grad, (1, 0))
+            sums.append(jnp.sum(jnp.where(diagonal, full, 0.0), axis=0, keepdims=True))
+        deltas[step] = jnp.concatenate(sums, axis=1)
+        return carry
+
+    lax.fori_loop(0, steps, raise_grads, 0)
 
     lat_copy.wait_recv()
     pos_copy.wait_recv()
@@ -120,35 +140,22 @@
         key_pos = jnp.broadcast_to(pos_in[half], (slots, slots)).T
         bias[cols, :] = jnp.where(key_pos <= query_pos, 0.0, -1e30)
     key_acc[...] = jnp.zeros_like(key_acc)
-    up_in.wait()
     q_in.wait()
     lse_in.wait()
-    diagonal = lax.broadcasted_iota(jnp.int32, (slots, slots), 0) == lax.broadcasted_iota(
-        jnp.int32, (slots, slots), 1)
-
-    def attend(pair):
-        one, two = 2 * pair, 2 * pair + 1
-        lat_grads, deltas = [], []
-        for head in (one, two):
-            lat_grad = dot(up_ref[head], grad_h[head], (1, 1)).astype(BF16)
-            lat_grads.append(lat_grad)
-            full = dot(saved_h[head], lat_grad, (1, 0))
-            deltas.append(jnp.sum(jnp.where(diagonal, full, 0.0), axis=0, keepdims=True))
-        lat_grad = jnp.concatenate(lat_grads, axis=1)
-        delta = jnp.concatenate(deltas, axis=1)
-        query = jnp.concatenate([q_ref[one], q_ref[two]], axis=1)
-        lse = jnp.concatenate([lse_ref[pl.ds(one, 1), :], lse_ref[pl.ds(two, 1), :]], axis=1)
-        mask = jnp.concatenate([bias[...], bias[...]], axis=1)
+
+    def attend(step):
+        members = [step * PER_STEP + offset for offset in range(PER_STEP)]
+        query = jnp.concatenate([q_ref[head] for head in members], axis=1)
+        lse = jnp.concatenate([lse_ref[pl.ds(head, 1), :] for head in members], axis=1)
+        mask = jnp.concatenate([bias[...]] * PER_STEP, axis=1)
+        lat_grad = lat_grads[step]
         logits = dot(keys[...], query, (1, 0)) * scaling
+        dot_value = dot(keys[:, :latent], lat_grad, (1, 0))
         weights = jnp.exp(logits - lse + mask)
-        dot_value = dot(keys[:, :latent], lat_grad, (1, 0))
-        dlogits = (weights * (dot_value - delta) * scaling).astype(BF16)
-        weights_b = weights.astype(BF16)
-        query_grad = dot(keys_t[...], dlogits, (1, 0)).astype(BF16)
-        qg_ref[one] = query_grad[:, :slots]
-        qg_ref[two] = query_grad[:, slots:]
+        dlogits = (weights * (dot_value - deltas[step]) * scaling).astype(BF16)
+        dlogits_all[step] = dlogits
         key_term = dot(query, dlogits, (1, 1))
-        value_term = dot(lat_grad, weights_b, (1, 1))
+        value_term = dot(lat_grad, weights.astype(BF16), (1, 1))
         key_acc[:latent, :] += key_term[:latent] + value_term
         key_acc[latent:width, :] += key_term[latent:]
 
@@ -167,56 +174,70 @@
         for step in range(1, n_dp):
             z_copy(step, chunk).start()
 
-    def attend_and_forward(pair, carry):
-        attend(pair)
-
-        @pl.when(pair >= 1)
-        def _():
-            forward(pair - 1)
-
-        return carry
-
-    lax.fori_loop(0, chunks, attend_and_forward, 0)
-    qg_copy = pltpu.make_async_copy(qg_ref, qg_hbm, out_sem)
-    qg_copy.start()
+    def attend_and_forward(step, carry):
+        attend(step)
+        for part in range(ratio):
+            chunk = step * ratio + part - 1
+
+            @pl.when(chunk >= 0)
+            def _():
+                forward(chunk)
+
+        return carry
+
+    lax.fori_loop(0, steps - 1, attend_and_forward, 0)
+    attend(steps - 1)
 
     for part in range(n_head):
         for ctx in range(2):
             ka_send[part, ctx] = key_acc[
                 part * piece:(part + 1) * piece, ctx * slots:(ctx + 1) * slots].astype(BF16)
-    ka_copies = []
-    for step in range(1, n_head):
-        to = lax.rem(my_head + step, n_head)
-        copy = send(ka_send.at[to], ka_recv.at[my_head], ka_ssem.at[to], ka_rsem.at[my_head], {"head": to})
-        copy.start()
-        ka_copies.append(copy)
-
-    forward(chunks - 1)
+
+    def ka_copy(step, arriving=False):
+        peer = lax.rem(my_head + step, n_head)
+        slot = peer if arriving else my_head
+        return send(ka_send.at[peer], ka_recv.at[slot], ka_ssem.at[peer], ka_rsem.at[slot], {"head": peer})
+
+    def kc_copy(step, arriving=False):
+        peer = lax.rem(my_head + step, n_head)
+        slot = peer if arriving else my_head
+        return send(kc.at[slot], kc.at[slot], kc_ssem.at[peer], kc_rsem.at[slot], {"head": peer})
+
+    for step in range(1, n_head):
+        ka_copy(step).start()
+
+    for part in range(ratio):
+        forward((steps - 1) * ratio + part - 1)
+
+    def query_grads(step, carry):
+        query_grad = dot(keys_t[...], dlogits_all[step], (1, 0)).astype(BF16)
+        for offset in range(PER_STEP):
+            qg_ref[step * PER_STEP + offset] = query_grad[:, offset * slots:(offset + 1) * slots]
+        return carry
+
+    lax.fori_loop(0, steps // 2, query_grads, 0)
 
     sums = ka_send[my_head].astype(F32)
     for step in range(1, n_head):
-        src = lax.rem(my_head + step, n_head)
-        send(ka_send.at[src], ka_recv.at[src], ka_ssem.at[src], ka_rsem.at[src], {"head": src}).wait_recv()
-        sums = sums + ka_recv[src].astype(F32)
+        ka_copy(step, arriving=True).wait_recv()
+        sums = sums + ka_recv[lax.rem(my_head + step, n_head)].astype(F32)
     kb_send[...] = sums.astype(BF16)
     kb_copy = send(kb_send.at[other], kb_recv, kb_sem.at[0], kb_sem.at[1], {"ctx": other})
     kb_copy.start()
 
+    lax.fori_loop(steps // 2, steps, query_grads, 0)
+    qg_copy = pltpu.make_async_copy(qg_ref, qg_hbm, out_sem.at[0])
+    qg_copy.start()
+    forward(chunks - 1)
+
     kb_copy.wait_recv()
     kc[my_head] = (kb_send[my_ctx].astype(F32) + kb_recv[...].astype(F32)).astype(BF16)
-    kc_copies = []
-    for step in range(1, n_head):
-        to = lax.rem(my_head + step, n_head)
-        copy = send(kc.at[my_head], kc.at[my_head], kc_ssem.at[to], kc_rsem.at[my_head], {"head": to})
-        copy.start()
-        kc_copies.append(copy)
-
-    for step in range(1, n_head):
-        src = lax.rem(my_head + step, n_head)
-        send(kc.at[src], kc.at[src], kc_ssem.at[src], kc_rsem.at[src], {"head": src}).wait_recv()
-    for part in range(n_head):
-        first, last = part * piece, min((part + 1) * piece, width)
-        lg_out[first:last, :] = kc[part, :last - first, :].astype(F32)
+    for step in range(1, n_head):
+        kc_copy(step).start()
+
+    def vg_copy(chunk):
+        part = pl.ds(chunk * PER_CHUNK, PER_CHUNK)
+        return pltpu.make_async_copy(vg_ref.at[part], vg_hbm.at[part], vg_sem.at[chunk])
 
     def finish(chunk, carry):
         for step in range(1, n_dp):
@@ -226,31 +247,63 @@
             total = zs[my_dp, head].astype(F32)
             for step in range(1, n_dp):
                 total = total + zr[lax.rem(my_dp + step, n_dp), head].astype(F32)
-            vg_out[pl.ds(head, share, heads), :] = total
-        return carry
-
-    lax.fori_loop(0, chunks, finish, 0)
+            vg_ref[head] = total
+        vg_copy(chunk).start()
+        return carry
+
+    lax.fori_loop(0, chunks - ratio, finish, 0)
+    for step in range(1, n_head):
+        kc_copy(step, arriving=True).wait_recv()
+    for part in range(n_head):
+        first, last = part * piece, min((part + 1) * piece, width)
+        lg_ref[first:last, :] = kc[part, :last - first, :].astype(F32)
+    lg_copy = pltpu.make_async_copy(lg_ref, lg_hbm, out_sem.at[1])
+    lg_copy.start()
+    lax.fori_loop(chunks - ratio, chunks, finish, 0)
 
     def drain(chunk, carry):
         x_copy(chunk).wait_send()
         for step in range(1, n_dp):
             z_copy(step, chunk).wait_send()
+        vg_copy(chunk).wait()
         return carry
 
     lax.fori_loop(0, chunks, drain, 0)
-    for copy in [lat_copy, pos_copy, kb_copy] + ka_copies + kc_copies:
+    for copy in [lat_copy, pos_copy, kb_copy]:
         copy.wait_send()
+    for step in range(1, n_head):
+        ka_copy(step).wait_send()
+        kc_copy(step).wait_send()
     qg_copy.wait()
-
-
-def write_out(*refs):
-    count = len(refs) // 2
-    sems = refs[-1]
-    copies = [pltpu.make_async_copy(refs[i], refs[count + i], sems.at[i]) for i in range(count)]
-    for copy in copies:
-        copy.start()
-    for copy in copies:
-        copy.wait()
+    lg_copy.wait()
+
+
+def write_out(qg_hbm, lg_hbm, vg_hbm, qg_out, lg_out, vg_out, qg_ref, lg_ref, vg_ref, vg_rows, in_sem, out_sem):
+    heads, share, _ = vg_ref.shape
+    come = pltpu.make_async_copy(vg_hbm, vg_ref, in_sem.at[0])
+    leave = pltpu.make_async_copy(vg_rows, vg_out, out_sem.at[0])
+    pieces = [(
+        pltpu.make_async_copy(lg_hbm, lg_ref, in_sem.at[1]),
+        pltpu.make_async_copy(lg_ref, lg_out, out_sem.at[1]))]
+    size = heads // 4
+    for part in range(4):
+        rows = pl.ds(part * size, size)
+        pieces.append((
+            pltpu.make_async_copy(qg_hbm.at[rows], qg_ref.at[rows], in_sem.at[2 + part]),
+            pltpu.make_async_copy(qg_ref.at[rows], qg_out.at[rows], out_sem.at[2 + part])))
+    come.start()
+    for first, _ in pieces:
+        first.start()
+    come.wait()
+    for head in range(heads):
+        vg_rows[pl.ds(head, share, heads), :] = vg_ref[head]
+    leave.start()
+    for first, second in pieces:
+        first.wait()
+        second.start()
+    leave.wait()
+    for _, second in pieces:
+        second.wait()
 
 
 def fused(mesh, queries, latents, positions, lse, saved_out, out_grad, value_up):
@@ -263,20 +316,16 @@
     piece = -(-width // unit) * 16
     dims = (n_dp, n_head, heads, slots, width, latent, share)
     dma = pltpu.SemaphoreType.DMA
-    chunks = heads // PER_CHUNK
+    chunks, steps = heads // PER_CHUNK, heads // PER_STEP
     results = pl.pallas_call(
         functools.partial(kernel, dims),
         out_shape=(
             jax.ShapeDtypeStruct((heads, width, slots), BF16),
             jax.ShapeDtypeStruct((width, slots), F32),
-            jax.ShapeDtypeStruct((share * heads, vhead), F32),
+            jax.ShapeDtypeStruct((heads, share, vhead), F32),
         ),
         in_specs=[pl.BlockSpec(memory_space=pltpu.HBM)] * 7,
-        out_specs=(
-            pl.BlockSpec(memory_space=pl.ANY),
-            pl.BlockSpec(memory_space=pltpu.VMEM),
-            pl.BlockSpec(memory_space=pltpu.VMEM),
-        ),
+        out_specs=(pl.BlockSpec(memory_space=pl.ANY),) * 3,
         scratch_shapes=[
             pltpu.VMEM((heads, width, slots), BF16),
             pltpu.VMEM((2, width, slots), BF16),
@@ -290,6 +339,9 @@
             pltpu.VMEM((slots * heads, vhead), F32),
             pltpu.VMEM((heads, slots, latent), BF16),
             pltpu.VMEM((heads, slots, vhead), BF16),
+            pltpu.VMEM((steps, latent, PER_STEP * slots), BF16),
+            pltpu.VMEM((steps, 1, PER_STEP * slots), F32),
+            pltpu.VMEM((steps, 2 * slots, PER_STEP * slots), BF16),
             pltpu.VMEM((2 * slots, width), BF16),
             pltpu.VMEM((width, 2 * slots), BF16),
             pltpu.VMEM((2 * slots, slots), F32),
@@ -304,6 +356,8 @@
             pltpu.VMEM((piece, slots), BF16),
             pltpu.VMEM((n_head, piece, slots), BF16),
             pltpu.VMEM((heads, width, slots), BF16),
+            pltpu.VMEM((width, slots), F32),
+            pltpu.VMEM((heads, share, vhead), F32),
             dma((7,)),
             dma((2,)), dma((2,)),
             dma((chunks,)), dma((chunks,)),
@@ -311,7 +365,7 @@
             dma((n_head,)), dma((n_head,)),
             dma((2,)),
             dma((n_head,)), dma((n_head,)),
-            dma,
+            dma((2,)), dma((chunks,)),
         ],
         compiler_params=pltpu.CompilerParams(
             collective_id=0, has_side_effects=True, vmem_limit_bytes=64 * 1024 * 1024),
@@ -326,10 +380,15 @@
     )
     query_grad, latent_grad, up_grad = pl.pallas_call(
         write_out,
-        out_shape=tuple(jax.ShapeDtypeStruct(r.shape, r.dtype) for r in results),
+        out_shape=(
+            jax.ShapeDtypeStruct((heads, width, slots), BF16),
+            jax.ShapeDtypeStruct((width, slots), F32),
+            jax.ShapeDtypeStruct((share * heads, vhead), F32),
+        ),
         in_specs=[pl.BlockSpec(memory_space=pl.ANY)] * 3,
         out_specs=(pl.BlockSpec(memory_space=pl.ANY),) * 3,
-        scratch_shapes=[dma((3,))],
+        scratch_shapes=[pltpu.VMEM(r.shape, r.dtype) for r in results] + [
+            pltpu.VMEM((share * heads, vhead), F32), dma((6,)), dma((6,))],
         compiler_params=pltpu.CompilerParams(vmem_limit_bytes=64 * 1024 * 1024),
     )(*results)
     return (

time: 79.7 us -> 30.5 us (0.38)
  Pallas kernels: 78.9 us -> 29.7 us
    pallas_call x1, Pallas kernels: 49.3 us -> 2.31 us  [fused(): pl.pallas_call(write_out, out_shape=(jax.ShapeDtypeStruct((heads, width,...]
    pallas_call x1, Pallas kernels: 29.6 us -> 27.4 us  [fused(): pl.pallas_call(functools.partial(kernel, dims), out_shape=(jax.ShapeDtype...]
where the time goes in v4:
time: 30.5 us; the launch traced here: 30.4 us
  Pallas kernels  29.7 us (97%)
  between operations  0.64 us (2%)
    pallas_call x1, Pallas kernels, fused(): pl.pallas_call(functools.partial(kernel, dims), out_shape=(jax.ShapeDtype...  27.4 us
    pallas_call x1, Pallas kernels, fused(): pl.pallas_call(write_out, out_shape=(jax.ShapeDtypeStruct((heads, width,...  2.31 us

profile of v4, /device:TPU:0, one launch (start us, length us, event | category | flops | bytes accessed | tf_op | source)
XLA Modules:
  0.0 30.4 jit_solution(8244015372646394553)
XLA Ops:
  0.6 27.4 %shard_map.94 = (bf16[16,288,128]{2,1,0:T(8,128)(2,1)}, f32[288,128]{1,0:T(8,128)}, f32[16,32,128]{2,1,0:T(8,128)}) custom-call(bf16[16,288,128]{2,1,0:T(8,128)(2,1)} %bitcast.18, bf16[288,128]{1,0:T(8,128)(2,1)} %bitcast.21, s32[1,128]{1,0:T(1,128)} %pos_hbm.1, f32[16,128]{1,0:T(8,128)} %bitcast.22, bf16[2048,256]{1,0:T(8,128)(2,1)} %bitcast.19, ...), custom_call_target="tpu_custom_call" | custom-call | tf_op jit(solution)/shard_map/pallas_call | solution.py:320
  28.1 2.3 %shard_map.95 = (bf16[16,288,128]{2,1,0:T(8,128)(2,1)}, f32[288,128]{1,0:T(8,128)}, f32[512,128]{1,0:T(8,128)}) custom-call(bf16[16,288,128]{2,1,0:T(8,128)(2,1)} %get-tuple-element.9.qg_hbm, f32[288,128]{1,0:T(8,128)} %get-tuple-element.10.lg_hbm, f32[16,32,128]{2,1,0:T(8,128)} %get-tuple-element.11.vg_hbm), custom_call_target="tpu_custom_call" | custom-call | tf_op jit(solution)/shard_map/pallas_call | solution.py:381

commit v5 on v3

--- a/solution.py
+++ b/solution.py
@@ -28,15 +28,15 @@
 def kernel(
     dims,
     q_hbm, lat_hbm, pos_hbm, lse_hbm, saved_hbm, grad_hbm, up_hbm,
-    qg_hbm, lg_out, vg_out,
+    qg_hbm, lg_hbm, vg_hbm,
     q_ref, kt_in, pos_in, lse_ref, saved_b, grad_b, up_ref,
     saved_lo, saved_hi, grad_f, lat_grads, deltas, dlogits_all,
     keys, keys_t, bias,
     vx, vr, zs, zr,
     key_acc, ka_send, ka_recv, kc,
-    qg_ref,
+    qg_ref, lg_ref, vg_ref,
     in_sem, lat_send, lat_recv, x_send, x_recv, z_send, z_recv,
-    ka_ssem, ka_rsem, kc_ssem, kc_rsem, out_sem,
+    ka_ssem, ka_rsem, kc_ssem, kc_rsem, out_sem, vg_sem,
 ):
     n_dp, n_head, heads, slots, width, latent, share = dims
     scaling = (VHEAD + ROPE) ** -0.5
@@ -54,31 +54,24 @@
     pos_load = load(1, pos_hbm, pos_in.at[my_ctx])
     saved_in = load(2, saved_hbm, saved_b)
     grad_in = load(3, grad_hbm, grad_b)
-    up_in = load(4, up_hbm, up_ref)
-    q_in = load(5, q_hbm, q_ref)
-    lse_in = load(6, lse_hbm, lse_ref)
 
     barrier = pltpu.get_barrier_semaphore()
     for step in range(1, n_dp):
         pl.semaphore_signal(barrier, inc=1, device_id={"dp": lax.rem(my_dp + step, n_dp)}, device_id_type=MESH)
-    for where in slab_peers(my_ctx, my_head, n_head):
+    peers = slab_peers(my_ctx, my_head, n_head)
+    for where in peers:
         pl.semaphore_signal(barrier, inc=1, device_id=where, device_id_type=MESH)
-    lat_in.wait()
-    pos_load.wait()
-    pl.semaphore_wait(barrier, (n_dp - 1) + (2 * n_head - 1))
 
     def send(source, target, send_sem, recv_sem, where):
         return pltpu.make_async_remote_copy(
             src_ref=source, dst_ref=target, send_sem=send_sem, recv_sem=recv_sem,
             device_id=where, device_id_type=MESH)
 
-    lat_copy = send(kt_in.at[my_ctx], kt_in.at[my_ctx], lat_send.at[0], lat_recv.at[0], {"ctx": other})
-    pos_copy = send(pos_in.at[my_ctx], pos_in.at[my_ctx], lat_send.at[1], lat_recv.at[1], {"ctx": other})
-    lat_copy.start()
-    pos_copy.start()
-
     saved_in.wait()
     grad_in.wait()
+    up_in = load(4, up_hbm, up_ref)
+    q_in = load(5, q_hbm, q_ref)
+    lse_in = load(6, lse_hbm, lse_ref)
     rows_step = (slots * heads) // 8
 
     def widen(step, carry):
@@ -89,6 +82,14 @@
         return carry
 
     lax.fori_loop(0, 8, widen, 0)
+
+    lat_in.wait()
+    pos_load.wait()
+    pl.semaphore_wait(barrier, (n_dp - 1) + (2 * n_head - 1))
+    lat_copy = send(kt_in.at[my_ctx], kt_in.at[my_ctx], lat_send.at[0], lat_recv.at[0], {"ctx": other})
+    pos_copy = send(pos_in.at[my_ctx], pos_in.at[my_ctx], lat_send.at[1], lat_recv.at[1], {"ctx": other})
+    lat_copy.start()
+    pos_copy.start()
 
     def x_copy(chunk):
         part = pl.ds(chunk * PER_CHUNK, PER_CHUNK)
@@ -172,9 +173,9 @@
     def attend_and_forward(chunk, carry):
         attend(chunk)
 
-        @pl.when(chunk < chunks - 1)
+        @pl.when(chunk == 1)
         def _():
-            forward(chunk)
+            forward(0)
 
         return carry
 
@@ -190,11 +191,10 @@
         slot = theirs if arriving else mine
         return send(ka_send.at[theirs], ka_recv.at[slot], ka_ssem.at[theirs], ka_rsem.at[slot], where)
 
-    peers = slab_peers(my_ctx, my_head, n_head)
     for where in peers:
         ka_copy(where).start()
 
-    forward(chunks - 1)
+    forward(1)
 
     def query_grads(chunk, carry):
         query_grad = dot(keys_t[...], dlogits_all[chunk], (1, 0)).astype(BF16)
@@ -203,7 +203,7 @@
         return carry
 
     lax.fori_loop(0, chunks, query_grads, 0)
-    qg_copy = pltpu.make_async_copy(qg_ref, qg_hbm, out_sem)
+    qg_copy = pltpu.make_async_copy(qg_ref, qg_hbm, out_sem.at[0])
     qg_copy.start()
 
     sums = ka_send[my_ctx, my_head].astype(F32)
@@ -218,6 +218,13 @@
         copy.start()
         kc_copies.append(copy)
 
+    for chunk in range(2, chunks):
+        forward(chunk)
+
+    def vg_copy(chunk):
+        part = pl.ds(chunk * PER_CHUNK, PER_CHUNK)
+        return pltpu.make_async_copy(vg_ref.at[part], vg_hbm.at[part], vg_sem.at[chunk])
+
     def finish(chunk, carry):
         for step in range(1, n_dp):
             z_copy(step, chunk, arriving=True).wait_recv()
@@ -226,49 +233,61 @@
             total = zs[my_dp, head].astype(F32)
             for step in range(1, n_dp):
                 total = total + zr[lax.rem(my_dp + step, n_dp), head].astype(F32)
-            vg_out[pl.ds(head, share, heads), :] = total
-        return carry
-
-    lax.fori_loop(0, chunks, finish, 0)
-
+            vg_ref[head] = total
+        vg_copy(chunk).start()
+        return carry
+
+    lax.fori_loop(0, chunks - 1, finish, 0)
     for step in range(1, n_head):
         src = lax.rem(my_head + step, n_head)
         send(kc.at[src], kc.at[src], kc_ssem.at[src], kc_rsem.at[src], {"head": src}).wait_recv()
     for part in range(n_head):
         first, last = part * piece, min((part + 1) * piece, width)
-        lg_out[first:last, :] = kc[part, :last - first, :].astype(F32)
+        lg_ref[first:last, :] = kc[part, :last - first, :].astype(F32)
+    lg_copy = pltpu.make_async_copy(lg_ref, lg_hbm, out_sem.at[1])
+    lg_copy.start()
+    lax.fori_loop(chunks - 1, chunks, finish, 0)
 
     def drain(chunk, carry):
         x_copy(chunk).wait_send()
         for step in range(1, n_dp):
             z_copy(step, chunk).wait_send()
+        vg_copy(chunk).wait()
         return carry
 
     lax.fori_loop(0, chunks, drain, 0)
     for copy in [lat_copy, pos_copy] + [ka_copy(where) for where in peers] + kc_copies:
         copy.wait_send()
     qg_copy.wait()
-
-
-def write_out(*refs):
-    sources, targets, rooms, (in_sem, out_sem) = refs[:3], refs[3:6], refs[6:9], refs[9:]
-    pieces = []
-    for source, target, room in zip(sources, targets, rooms):
-        count = 4 if source.ndim == 3 else 1
-        size = source.shape[0] // count
-        for part in range(count):
-            rows = pl.ds(part * size, size)
-            index = len(pieces)
-            pieces.append((
-                pltpu.make_async_copy(source.at[rows], room.at[rows], in_sem.at[index]),
-                pltpu.make_async_copy(room.at[rows], target.at[rows], out_sem.at[index])))
-    for come, _ in pieces:
-        come.start()
-    for come, leave in pieces:
-        come.wait()
-        leave.start()
-    for _, leave in pieces:
-        leave.wait()
+    lg_copy.wait()
+
+
+def write_out(qg_hbm, lg_hbm, vg_hbm, qg_out, lg_out, vg_out, qg_ref, lg_ref, vg_ref, vg_rows, in_sem, out_sem):
+    heads, share, _ = vg_ref.shape
+    come = pltpu.make_async_copy(vg_hbm, vg_ref, in_sem.at[0])
+    leave = pltpu.make_async_copy(vg_rows, vg_out, out_sem.at[0])
+    pieces = [(
+        pltpu.make_async_copy(lg_hbm, lg_ref, in_sem.at[1]),
+        pltpu.make_async_copy(lg_ref, lg_out, out_sem.at[1]))]
+    size = heads // 4
+    for part in range(4):
+        rows = pl.ds(part * size, size)
+        pieces.append((
+            pltpu.make_async_copy(qg_hbm.at[rows], qg_ref.at[rows], in_sem.at[2 + part]),
+            pltpu.make_async_copy(qg_ref.at[rows], qg_out.at[rows], out_sem.at[2 + part])))
+    come.start()
+    for first, _ in pieces:
+        first.start()
+    come.wait()
+    for head in range(heads):
+        vg_rows[pl.ds(head, share, heads), :] = vg_ref[head]
+    leave.start()
+    for first, second in pieces:
+        first.wait()
+        second.start()
+    leave.wait()
+    for _, second in pieces:
+        second.wait()
 
 
 def fused(mesh, queries, latents, positions, lse, saved_out, out_grad, value_up):
@@ -287,14 +306,10 @@
         out_shape=(
             jax.ShapeDtypeStruct((heads, width, slots), BF16),
             jax.ShapeDtypeStruct((width, slots), F32),
-            jax.ShapeDtypeStruct((share * heads, vhead), F32),
+            jax.ShapeDtypeStruct((heads, share, vhead), F32),
         ),
         in_specs=[pl.BlockSpec(memory_space=pltpu.HBM)] * 7,
-        out_specs=(
-            pl.BlockSpec(memory_space=pl.ANY),
-            pl.BlockSpec(memory_space=pltpu.VMEM),
-            pl.BlockSpec(memory_space=pltpu.VMEM),
-        ),
+        out_specs=(pl.BlockSpec(memory_space=pl.ANY),) * 3,
         scratch_shapes=[
             pltpu.VMEM((heads, width, slots), BF16),
             pltpu.VMEM((2, width, slots), BF16),
@@ -321,13 +336,15 @@
             pltpu.VMEM((2, n_head, piece, slots), BF16),
             pltpu.VMEM((n_head, piece, slots), BF16),
             pltpu.VMEM((heads, width, slots), BF16),
+            pltpu.VMEM((width, slots), F32),
+            pltpu.VMEM((heads, share, vhead), F32),
             dma((7,)),
             dma((2,)), dma((2,)),
             dma((chunks,)), dma((chunks,)),
             dma((n_dp, chunks)), dma((n_dp, chunks)),
             dma((2, n_head)), dma((2, n_head)),
             dma((n_head,)), dma((n_head,)),
-            dma,
+            dma((2,)), dma((chunks,)),
         ],
         compiler_params=pltpu.CompilerParams(
             collective_id=0, has_side_effects=True, vmem_limit_bytes=64 * 1024 * 1024),
@@ -342,10 +359,15 @@
     )
     query_grad, latent_grad, up_grad = pl.pallas_call(
         write_out,
-        out_shape=tuple(jax.ShapeDtypeStruct(r.shape, r.dtype) for r in results),
+        out_shape=(
+            jax.ShapeDtypeStruct((heads, width, slots), BF16),
+            jax.ShapeDtypeStruct((width, slots), F32),
+            jax.ShapeDtypeStruct((share * heads, vhead), F32),
+        ),
         in_specs=[pl.BlockSpec(memory_space=pl.ANY)] * 3,
         out_specs=(pl.BlockSpec(memory_space=pl.ANY),) * 3,
-        scratch_shapes=[pltpu.VMEM(r.shape, r.dtype) for r in results] + [dma((6,)), dma((6,))],
+        scratch_shapes=[pltpu.VMEM(r.shape, r.dtype) for r in results] + [
+            pltpu.VMEM((share * heads, vhead), F32), dma((6,)), dma((6,))],
         compiler_params=pltpu.CompilerParams(vmem_limit_bytes=64 * 1024 * 1024),
     )(*results)
     return (

time: 29.5 us -> 34.1 us (1.16)
  Pallas kernels: 28.8 us -> 33.3 us
    pallas_call x1, Pallas kernels: 26.5 us -> 31 us  [fused(): pl.pallas_call(functools.partial(kernel, dims), out_shape=(jax.ShapeDtype...]
where the time goes in v5:
time: 34.1 us; the launch traced here: 33.9 us
  Pallas kernels  33.3 us (98%)
  between operations  0.64 us (2%)
    pallas_call x1, Pallas kernels, fused(): pl.pallas_call(functools.partial(kernel, dims), out_shape=(jax.ShapeDtype...  31 us
    pallas_call x1, Pallas kernels, fused(): pl.pallas_call(write_out, out_shape=(jax.ShapeDtypeStruct((heads, width,...  2.31 us

profile of v5, /device:TPU:0, one launch (start us, length us, event | category | flops | bytes accessed | tf_op | source)
XLA Modules:
  0.0 33.9 jit_solution(963910733095938675)
XLA Ops:
  0.6 31.0 %shard_map.94 = (bf16[16,288,128]{2,1,0:T(8,128)(2,1)}, f32[288,128]{1,0:T(8,128)}, f32[16,32,128]{2,1,0:T(8,128)}) custom-call(bf16[16,288,128]{2,1,0:T(8,128)(2,1)} %bitcast.18, bf16[288,128]{1,0:T(8,128)(2,1)} %bitcast.21, s32[1,128]{1,0:T(1,128)} %pos_hbm.1, f32[16,128]{1,0:T(8,128)} %bitcast.22, bf16[2048,256]{1,0:T(8,128)(2,1)} %bitcast.19, ...), custom_call_target="tpu_custom_call" | custom-call | tf_op jit(solution)/shard_map/pallas_call | solution.py:304
  31.6 2.3 %shard_map.95 = (bf16[16,288,128]{2,1,0:T(8,128)(2,1)}, f32[288,128]{1,0:T(8,128)}, f32[512,128]{1,0:T(8,128)}) custom-call(bf16[16,288,128]{2,1,0:T(8,128)(2,1)} %get-tuple-element.9.qg_hbm, f32[288,128]{1,0:T(8,128)} %get-tuple-element.10.lg_hbm, f32[16,32,128]{2,1,0:T(8,128)} %get-tuple-element.11.vg_hbm), custom_call_target="tpu_custom_call" | custom-call | tf_op jit(solution)/shard_map/pallas_call | solution.py:360

commit v6 on v3

--- a/solution.py
+++ b/solution.py
@@ -154,11 +154,13 @@
         key_acc[:latent, :] += key_term[:latent] + value_term
         key_acc[latent:width, :] += key_term[latent:]
 
-    def z_copy(step, chunk, arriving=False):
-        peer = lax.rem(my_dp + step, n_dp)
+    near = my_dp + 1 - 2 * lax.rem(my_dp, 2)
+    far = lax.rem(my_dp + 2, n_dp)
+
+    def z_copy(slot, chunk):
         part = pl.ds(chunk * PER_CHUNK, PER_CHUNK)
-        slot = peer if arriving else my_dp
-        return send(zs.at[peer, part], zr.at[slot, part], z_send.at[peer, chunk], z_recv.at[slot, chunk], {"dp": peer})
+        piece_at, to = ((near, near), (lax.rem(near + 2, n_dp), near), (far, far))[slot]
+        return send(zs.at[piece_at, part], zr.at[slot, part], z_send.at[slot, chunk], z_recv.at[slot, chunk], {"dp": to})
 
     def forward(chunk):
         x_copy(chunk).wait_recv()
@@ -166,8 +168,15 @@
             head = chunk * PER_CHUNK + offset
             for dp in range(n_dp):
                 zs[dp, head] = (vx[my_ctx, head, dp].astype(F32) + vr[head, dp].astype(F32)).astype(BF16)
-        for step in range(1, n_dp):
-            z_copy(step, chunk).start()
+        z_copy(1, chunk).start()
+        z_copy(0, chunk).start()
+
+    def pass_on(chunk):
+        z_copy(1, chunk).wait_recv()
+        for offset in range(PER_CHUNK):
+            head = chunk * PER_CHUNK + offset
+            zs[far, head] = (zs[far, head].astype(F32) + zr[1, head].astype(F32)).astype(BF16)
+        z_copy(2, chunk).start()
 
     def attend_and_forward(chunk, carry):
         attend(chunk)
@@ -175,6 +184,10 @@
         @pl.when(chunk < chunks - 1)
         def _():
             forward(chunk)
+
+        @pl.when((chunk >= 1) & (chunk < chunks - 1))
+        def _():
+            pass_on(chunk - 1)
 
         return carry
 
@@ -195,6 +208,7 @@
         ka_copy(where).start()
 
     forward(chunks - 1)
+    pass_on(chunks - 2)
 
     def query_grads(chunk, carry):
         query_grad = dot(keys_t[...], dlogits_all[chunk], (1, 0)).astype(BF16)
@@ -218,14 +232,15 @@
         copy.start()
         kc_copies.append(copy)
 
+    pass_on(chunks - 1)
+
     def finish(chunk, carry):
-        for step in range(1, n_dp):
-            z_copy(step, chunk, arriving=True).wait_recv()
+        z_copy(0, chunk).wait_recv()
+        z_copy(2, chunk).wait_recv()
         for offset in range(PER_CHUNK):
             head = chunk * PER_CHUNK + offset
             total = zs[my_dp, head].astype(F32)
-            for step in range(1, n_dp):
-                total = total + zr[lax.rem(my_dp + step, n_dp), head].astype(F32)
+            total = total + zr[0, head].astype(F32) + zr[2, head].astype(F32)
             vg_out[pl.ds(head, share, heads), :] = total
         return carry
 
@@ -240,8 +255,8 @@
 
     def drain(chunk, carry):
         x_copy(chunk).wait_send()
-        for step in range(1, n_dp):
-            z_copy(step, chunk).wait_send()
+        for slot in range(3):
+            z_copy(slot, chunk).wait_send()
         return carry
 
     lax.fori_loop(0, chunks, drain, 0)
@@ -430,7 +445,7 @@
 
 
 def solution(mesh):
-    body = functools.partial(fused, mesh) if mesh.shape["ctx"] == 2 else spread
+    body = functools.partial(fused, mesh) if (mesh.shape["ctx"], mesh.shape["dp"]) == (2, 4) else spread
     return jax.shard_map(
         body,
         mesh=mesh,

time: 29.5 us -> 31.3 us (1.061)
  Pallas kernels: 28.8 us -> 30.5 us
    pallas_call x1, Pallas kernels: 26.5 us -> 28.3 us  [fused(): pl.pallas_call(functools.partial(kernel, dims), out_shape=(jax.ShapeDtype...]
where the time goes in v6:
time: 31.3 us; the launch traced here: 31.2 us
  Pallas kernels  30.5 us (97%)
  between operations  0.64 us (2%)
    pallas_call x1, Pallas kernels, fused(): pl.pallas_call(functools.partial(kernel, dims), out_shape=(jax.ShapeDtype...  28.3 us
    pallas_call x1, Pallas kernels, fused(): pl.pallas_call(write_out, out_shape=tuple((jax.ShapeDtypeStruct(r.shape,...  2.21 us

profile of v6, /device:TPU:0, one launch (start us, length us, event | category | flops | bytes accessed | tf_op | source)
XLA Modules:
  0.0 31.2 jit_solution(6916887212713391660)
XLA Ops:
  0.6 28.3 %shard_map.94 = (bf16[16,288,128]{2,1,0:T(8,128)(2,1)}, f32[288,128]{1,0:T(8,128)}, f32[512,128]{1,0:T(8,128)}) custom-call(bf16[16,288,128]{2,1,0:T(8,128)(2,1)} %bitcast.18, bf16[288,128]{1,0:T(8,128)(2,1)} %bitcast.21, s32[1,128]{1,0:T(1,128)} %pos_hbm.1, f32[16,128]{1,0:T(8,128)} %bitcast.22, bf16[2048,256]{1,0:T(8,128)(2,1)} %bitcast.19, ...), custom_call_target="tpu_custom_call" | custom-call | tf_op jit(solution)/shard_map/pallas_call | solution.py:300
  29.0 2.2 %shard_map.95 = (bf16[16,288,128]{2,1,0:T(8,128)(2,1)}, f32[288,128]{1,0:T(8,128)}, f32[512,128]{1,0:T(8,128)}) custom-call(bf16[16,288,128]{2,1,0:T(8,128)(2,1)} %get-tuple-element.9.refs_0_, f32[288,128]{1,0:T(8,128)} %get-tuple-element.10.refs_1_, f32[512,128]{1,0:T(8,128)} %get-tuple-element.11.refs_2_), custom_call_target="tpu_custom_call" | custom-call | tf_op jit(solution)/shard_map/pallas_call | solution.py:358
